TPU v7x, 256 devices: a whole 4x4x8 slice. The times are simulated.
256 devices in a mesh: seq: 8 (over x_lo, y), dp: 32 (over x_hi, z, core).
Axes of the slice: x: 4 (x_hi: 2, x_lo: 2; x = x_hi * 2 + x_lo), y: 4, z: 8, core: 2. Of those that a mesh axis runs over, the one named last changes fastest.
Arguments:
- tokens: bfloat16 [32768, 1536], P(('dp', 'seq')), parts along dimension 0, may hold values from -6 to 6
- dilations: int32 [2], replicated, may hold values from 1 to 128, as said below
- taps: float32 [2, 3, 1536], replicated, may hold values from -3 to 3
- w_query: bfloat16 [1536, 512], replicated, may hold values from -0.15625 to 0.15625
- w_keyval: bfloat16 [1536, 256], replicated, may hold values from -0.15625 to 0.15625
- w_out: bfloat16 [512, 1536], replicated, may hold values from -0.25 to 0.25
- exponents: int32 [256], P(('dp', 'seq')), parts along dimension 0, may hold values from -9 to -6
- pair: bfloat16 [2048, 64, 128], P(('dp', 'seq')), parts along dimension 0
- w_bias: float32 [128, 4], replicated
- cotangent: bfloat16 [32768, 1536], P(('dp', 'seq')), parts along dimension 0, may hold values from -6 to 6
Outputs:
- output: bfloat16 [32768, 1536], P(('dp', 'seq')), parts along dimension 0
- grad_tokens: bfloat16 [32768, 1536], P(('dp', 'seq')), parts along dimension 0
- grad_query: bfloat16 [49152, 512], P(('dp', 'seq')), parts along dimension 0
- grad_keyval: bfloat16 [49152, 256], P(('dp', 'seq')), parts along dimension 0
- grad_out: bfloat16 [16384, 1536], P(('dp', 'seq')), parts along dimension 0
There are 32 independent parts, one for each index of `dp`. A program takes and returns all parts, laid end to end along the dimension named above; an argument that names none is the same for every part. Nothing has to cross between parts.
Inputs may be any that keep to these rules, and one draw needn't show every extreme that they name: One of the dilations equals 128.
All inputs are finite; a program needn't handle non-finite values.
Results may differ from a plain program's by a relative error of at most 0.025.
The roundings to bfloat16 on the way count: a program that leaves them out, or rounds other values in their place, can miss the bound.
Values may be sent and summed in bfloat16 or wider, within the bound.
No kernel may reach another device: no remote copies, remote signals or barrier semaphores. Data moves between devices by JAX's collectives and lax.ppermute only.
A program may use at most 64 MiB of HBM per device.

v0:
```python
import jax
import jax.numpy as jnp
from jax import lax
from jax.experimental import pallas as pl
from jax.experimental.pallas import tpu as pltpu
from jax.sharding import PartitionSpec as P

POOL = 16
CLIP_LEVEL = 448.0
RUN = 8
CONV_LIMIT = 63
F32 = jnp.float32
BF16 = jnp.bfloat16
MIB = 1 << 20
VMEM = pl.BlockSpec(memory_space=pltpu.VMEM)
SMEM = pl.BlockSpec(memory_space=pltpu.SMEM)
ANY = pl.BlockSpec(memory_space=pl.ANY)


def nn(a, b):
    return jnp.dot(a, b, preferred_element_type=F32)


def nt(a, b):
    return lax.dot_general(a, b, (((1,), (1,)), ((), ())), preferred_element_type=F32)


def call(body, outs, name, flops=0, nbytes=0, scratch=(), limit=16, space=VMEM):
    def run(*args):
        return pl.pallas_call(
            body,
            out_shape=[jax.ShapeDtypeStruct(s, d) for s, d in outs],
            in_specs=[SMEM if a.dtype == jnp.int32 else space for a in args],
            out_specs=[space] * len(outs),
            scratch_shapes=list(scratch),
            compiler_params=pltpu.CompilerParams(vmem_limit_bytes=limit * MIB),
            cost_estimate=pl.CostEstimate(flops=flops, bytes_accessed=nbytes, transcendentals=0),
            name=name,
        )(*args)

    return run


def exchange(x):
    return lax.all_to_all(x, "seq", split_axis=0, concat_axis=0, tiled=True)


def after(x, *others):
    return lax.optimization_barrier((x, *others))[0]


def flip_body(tok_hbm, cot_hbm, out_hbm, tok_ref, cot_ref, out_ref, sems):
    n, rows, _ = out_ref.shape
    half = rows // 2
    reads = [
        pltpu.make_async_copy(tok_hbm, tok_ref, sems.at[n]),
        pltpu.make_async_copy(cot_hbm, cot_ref, sems.at[n + 1]),
    ]
    for copy in reads:
        copy.start()
    reads[0].wait()
    for r in range(n):
        out_ref[r, :half, :] = tok_ref[:, r * half : (r + 1) * half].astype(F32).T.astype(BF16)
    reads[1].wait()
    writes = []
    for r in range(n):
        out_ref[r, half:, :] = cot_ref[:, r * half : (r + 1) * half].astype(F32).T.astype(BF16)
        writes.append(pltpu.make_async_copy(out_ref.at[r], out_hbm.at[r], sems.at[r]))
        writes[r].start()
    for copy in writes:
        copy.wait()


def split3(x):
    hi = x.astype(BF16)
    rest = x - hi.astype(F32)
    mid = rest.astype(BF16)
    lo = (rest - mid.astype(F32)).astype(BF16)
    return hi, mid, lo


def take_taps(me, taps_ref, turn_ref):
    begin = me * 192
    window = begin // 128 * 128
    for k in range(3):
        part = taps_ref[k, :, pl.ds(pl.multiple_of(window, 128), 256)]
        for layer in range(2):
            turn_ref[:, 8 * layer + k : 8 * layer + k + 1] = part[layer : layer + 1, :].T
    return begin - window


def early_body(exp_ref, cot_ref, wout_ref, pair_ref, wb_ref, out_ref):
    weights = jnp.concatenate([wb_ref[...], wb_ref[...]], axis=0).T
    lane = lax.broadcasted_iota(jnp.int32, (128, 128), 1)
    head = (lane % 32) // 8
    wide = jnp.zeros((128, 128), F32)
    for h in range(4):
        wide = jnp.where(head == h, weights[:, h : h + 1], wide)
    pieces = split3(wide)
    cells = jnp.zeros((64, 128), F32)
    for j in range(8):
        pick = lane % 8 == j
        for piece in pieces:
            cells += nn(pair_ref[j], jnp.where(pick, piece.astype(F32), 0.0).astype(BF16))
    hi, mid, lo = (piece.astype(F32) for piece in split3(cells))
    group = lax.broadcasted_iota(jnp.int32, (64, 128), 1) // 32
    factor, _ = power_of_two(exp_ref[0])
    packed = jnp.where(group == 0, hi, jnp.where(group == 1, mid, jnp.where(group == 2, lo, factor)))
    out_ref[512:, :] = packed.astype(BF16)
    grad = nt(cot_ref[...], wout_ref[...]).astype(BF16)
    for h in range(4):
        out_ref[128 * h : 128 * h + 128, :] = grad[:, 128 * h : 128 * h + 128]


def sigmoid(v):
    return 0.5 * jnp.tanh(0.5 * v) + 0.5


def shifts(blocks, d):
    lane = lax.broadcasted_iota(jnp.int32, blocks[0].shape, 1)
    turn = lax.rem(d, 128)
    back = 128 - d
    rolled = [pltpu.roll(b, turn, 1) for b in blocks]
    other = [pltpu.roll(b, back, 1) for b in blocks]
    zero = jnp.zeros_like(blocks[0])
    count = len(blocks)
    before = [
        jnp.where(lane < d, rolled[s - 1] if s else zero, rolled[s]) for s in range(count)
    ]
    after = [
        jnp.where(lane >= back, other[s + 1] if s + 1 < count else zero, other[s])
        for s in range(count)
    ]
    return before, after


def conv_body(dil_ref, me_ref, x_ref, taps_ref, out_ref, slope_ref, turn_ref):
    offset = take_taps(me_ref[0], taps_ref, turn_ref)
    count, channels, _ = out_ref.shape

    def chunk(c, carry):
        rows = pl.ds(pl.multiple_of(c * 16, 16), 16)
        cur = [x_ref[s, rows, :].astype(F32) for s in range(count)]
        tap = turn_ref[pl.ds(pl.multiple_of(offset + c * 16, 16), 16), :]
        for layer in range(2):
            t0, t1, t2 = (tap[:, 8 * layer + k : 8 * layer + k + 1] for k in range(3))
            before, after = shifts(cur, dil_ref[layer])
            for s in range(count):
                mixed = t0 * before[s] + t1 * cur[s] + t2 * after[s]
                sigma = sigmoid(mixed)
                gated = mixed * sigma
                slope_ref[layer, s, rows, :] = (sigma + gated * (1.0 - sigma)).astype(BF16)
                cur[s] = (cur[s] + gated).astype(BF16).astype(F32)
        for s in range(count):
            out_ref[s, rows, :] = cur[s].astype(BF16)
        return carry

    lax.fori_loop(0, channels // 16, chunk, 0)


def power_of_two(e):
    up, down = F32(1.0), F32(1.0)
    size = jnp.abs(e)
    for bit in range(6):
        on = ((size >> bit) & 1) == 1
        up = up * jnp.where(on, F32(2.0 ** (1 << bit)), F32(1.0))
        down = down * jnp.where(on, F32(0.5 ** (1 << bit)), F32(1.0))
    return jnp.where(e >= 0, up, down), jnp.where(e >= 0, down, up)


def keyval_body(exp_ref, x_ref, wkv_ref, wq_ref, send_ref, trunk_ref):
    count, channels, _ = x_ref.shape
    for s in range(count):
        trunk_ref[:, s * channels : (s + 1) * channels] = x_ref[s].astype(F32).T.astype(BF16)
    factor, inverse = power_of_two(exp_ref[0])
    unscaled = nn(trunk_ref[...], wkv_ref[...]) * inverse
    codes = jnp.clip(unscaled, -CLIP_LEVEL, CLIP_LEVEL).astype(BF16).astype(F32)
    marked = jnp.where(
        jnp.abs(unscaled) < CLIP_LEVEL, codes, jnp.where(unscaled > 0.0, F32(512.0), F32(-512.0))
    )
    marked = (marked * factor).astype(BF16)
    query = nn(trunk_ref[...], wq_ref[...]).astype(BF16)
    for s in range(count):
        send_ref[s, :, :256] = marked
        send_ref[s, :, 256:] = query


def query_body(me_ref, *refs):
    columns, (pack_ref, cells_ref) = refs[:8], refs[8:]
    me = me_ref[0]
    x, y = me // 4, lax.rem(me, 4)
    count = cells_ref.shape[0]
    for k, ref in enumerate(columns):
        block = (x if k < 4 else 1 - x) * 4 + lax.rem(y + (0, 3, 1, 2)[k % 4], 4)
        cells_ref[block] = ref[512:, :]
        pack_ref[block, :512, :] = ref[:512, :]
    row = lax.broadcasted_iota(jnp.int32, (128, 512), 0)
    col = lax.broadcasted_iota(jnp.int32, (128, 512), 1)
    same_head = (row % 32) // 8 == col // 128
    target = (row % 8) - (col % 64)
    mirrored = jnp.zeros((64, 512), F32)
    for s in range(count):
        pick = jnp.where(same_head & (row < 96) & (target == -8 * s), F32(1.0), F32(0.0))
        mirrored += nn(cells_ref[s], pick.astype(BF16))
    lane = lax.broadcasted_iota(jnp.int32, (64, 128), 1)
    for h in range(4):
        one = mirrored[:, 128 * h : 128 * h + 128]
        other = jnp.concatenate([one, one], axis=0).T
        bias = 0.5 * (one + other[:64, :]) * F32(128.0**0.5)
        hi = bias.astype(BF16).astype(F32)
        both = jnp.where(lane < 64, hi, bias - hi).astype(BF16)
        for s in range(count):
            wide = both[8 * s : 8 * s + 8].astype(F32)
            wide = jnp.broadcast_to(wide[:, None, :], (8, POOL, 128)).reshape(128, 128)
            pack_ref[s, 512 + 128 * h : 640 + 128 * h, :] = wide.astype(BF16)
    for s in range(count):
        corner = cells_ref[s, 0:1, 127:128].astype(F32)
        pack_ref[s, 1024:, :] = jnp.broadcast_to(corner, (16, 128)).astype(BF16)


def attention_body(
    kv_ref, pack_ref, att_ref, gq_ref, out_ref,
    sum_ref, kx_ref, v_ref, kt_ref, vt_ref, qx_ref, s_ref, sl_ref, pb_ref, cb_ref,
):
    scale = F32(128.0**-0.5)
    count = kv_ref.shape[0]
    length = count * 128
    for s in range(count):
        rows = slice(128 * s, 128 * s + 128)
        level = pack_ref[s, 1024:1025, 0:1].astype(F32) * CLIP_LEVEL
        plain = jnp.clip(kv_ref[s, :, :256].astype(F32), -level, level)
        kx_ref[rows, :128] = plain[:, :128].astype(BF16)
        v_ref[rows, :] = plain[:, 128:].astype(BF16)
        kt_ref[:, rows] = plain[:, :128].T.astype(BF16)
        vt_ref[:, rows] = plain[:, 128:].T.astype(BF16)
        for h in range(4):
            here = slice(128 * h, 128 * h + 128)
            qx_ref[s, here, :128] = kv_ref[s, :, 256 + 128 * h : 384 + 128 * h]
            qx_ref[s, here, 128:] = pack_ref[s, 512 + 128 * h : 640 + 128 * h, :]
    row = lax.broadcasted_iota(jnp.int32, (length, 128), 0)
    lane = lax.broadcasted_iota(jnp.int32, (length, 128), 1)
    kx_ref[:, 128:] = jnp.where(lane % 64 == row // POOL, F32(1.0), F32(0.0)).astype(BF16)
    sum_ref[...] = jnp.zeros_like(sum_ref)

    size = 256
    pieces = [slice(c * size, (c + 1) * size) for c in range(length // size)]
    fold = (size // 8, 8, 512)

    def scores(b, i):
        top = None
        for r in pieces:
            part = nt(kx_ref[r, :], qx_ref[i])
            s_ref[b, r, :] = part
            part = jnp.max(part.reshape(fold), axis=0)
            top = part if top is None else jnp.maximum(top, part)
        return jnp.max(top, axis=0, keepdims=True)

    def weigh(b, i, top):
        total = mean = jnp.zeros((8, 512), F32)
        for r in pieces:
            weights = jnp.exp2((s_ref[b, r, :] - top) * (scale * F32(1.4426950408889634)))
            slope = nt(v_ref[r, :], pack_ref[i, :512, :])
            s_ref[b, r, :] = weights
            sl_ref[b, r, :] = slope
            total += jnp.sum(weights.reshape(fold), axis=0)
            mean += jnp.sum((weights * slope).reshape(fold), axis=0)
        inverse = 1.0 / jnp.sum(total, axis=0, keepdims=True)
        return inverse, jnp.sum(mean, axis=0, keepdims=True) * inverse

    def products(b, i, inverse, mean):
        query, grad = qx_ref[i][:, :128], pack_ref[i, :512, :]
        for r in pieces:
            probs = s_ref[b, r, :] * inverse
            probs_b = probs.astype(BF16)
            centred_b = (probs * (sl_ref[b, r, :] - mean)).astype(BF16)
            pb_ref[b, r, :] = probs_b
            cb_ref[b, r, :] = centred_b
            sum_ref[r, :128] += nn(centred_b, query)
            sum_ref[r, 128:] += nn(probs_b, grad)
        attended = nn(vt_ref[...], pb_ref[b]).astype(BF16)
        grad_q = (nn(kt_ref[...], cb_ref[b]) * scale).astype(BF16)
        for h in range(4):
            here = slice(128 * h, 128 * h + 128)
            att_ref[i, here, :] = attended[:, here]
            gq_ref[i, here, :] = grad_q[:, here]

    def step(part, carry):
        start = part * RUN
        stats = weigh(0, start, scores(0, start))
        for d in range(RUN):
            last = d == RUN - 1
            top = None if last else scores((d + 1) % 2, start + d + 1)
            products(d % 2, start + d, *stats)
            if not last:
                stats = weigh((d + 1) % 2, start + d + 1, top)
        return carry

    lax.fori_loop(0, count // RUN, step, 0)
    side = lax.broadcasted_iota(jnp.int32, (128, 256), 1)
    for s in range(count):
        level = pack_ref[s, 1024:1025, 0:1].astype(F32) * CLIP_LEVEL
        inside = jnp.abs(kv_ref[s, :, :256].astype(F32)) <= level
        part = sum_ref[128 * s : 128 * s + 128, :]
        part = jnp.where(side < 128, part * scale, part)
        out_ref[s] = jnp.where(inside, part, 0.0).astype(BF16)


def output_body(me_ref, trunk_ref, att_ref, wout_ref, out_ref):
    me = me_ref[0]
    total = trunk_ref[...].astype(F32)
    for h in range(4):
        here = slice(128 * h, 128 * h + 128)
        total += nn(att_ref[me, here, :].astype(F32).T.astype(BF16), wout_ref[here, :])
    out_ref[...] = total.astype(BF16)


def back_body(
    dil_ref, me_ref, x_ref, att_ref, gq_ref, gkv_ref, wq_ref, wkv_ref, taps_ref, slope_ref,
    out_ref, g_ref, turn_ref,
):
    offset = take_taps(me_ref[0], taps_ref, turn_ref)
    count, channels, _ = g_ref.shape
    mine = pl.ds(pl.multiple_of(me_ref[0] * channels, 16), channels)
    my_wq, my_wkv = wq_ref[mine, :], wkv_ref[mine, :]
    grad_out = jnp.zeros((channels, 512), F32)
    for s in range(count):
        turned = x_ref[s, channels:, :]
        g_ref[s] = turned.astype(F32) + nn(my_wq, gq_ref[s]) + nt(my_wkv, gkv_ref[s])
        grad_out += nt(turned, att_ref[s])
    half = channels // 2
    for s in range(count):
        cols = grad_out[:, 64 * s : 64 * s + 64]
        out_ref[s, channels:, :] = jnp.concatenate([cols[:half], cols[half:]], axis=1).astype(BF16)

    def chunk(c, carry):
        rows = pl.ds(pl.multiple_of(c * 16, 16), 16)
        flow = [g_ref[s, rows, :] for s in range(count)]
        tap = turn_ref[pl.ds(pl.multiple_of(offset + c * 16, 16), 16), :]
        for layer in (1, 0):
            t0, t1, t2 = (tap[:, 8 * layer + k : 8 * layer + k + 1] for k in range(3))
            pushed = [
                (flow[s] * slope_ref[layer, s, rows, :].astype(F32)).astype(BF16).astype(F32)
                for s in range(count)
            ]
            before, after = shifts(pushed, dil_ref[layer])
            flow = [
                flow[s] + t0 * after[s] + t1 * pushed[s] + t2 * before[s] for s in range(count)
            ]
        for s in range(count):
            out_ref[s, rows, :] = flow[s].astype(BF16)
        return carry

    lax.fori_loop(0, channels // 16, chunk, 0)


def weights_body(x_ref, gq_ref, gkv_ref, gq_out_ref, gkv_out_ref):
    count, channels, _ = x_ref.shape
    first = jnp.zeros(gq_out_ref.shape, F32)
    second = jnp.zeros(gkv_out_ref.shape, F32)
    for s in range(count):
        first += nt(x_ref[s], gq_ref[s])
        second += nn(x_ref[s], gkv_ref[s])
    gq_out_ref[...] = first.astype(BF16)
    gkv_out_ref[...] = second.astype(BF16)


def last_body(x_ref, grad_ref, gout_ref):
    count, wide, _ = x_ref.shape
    channels = grad_ref.shape[1] // count
    half = wide - channels
    for s in range(count):
        grad_ref[:, s * channels : (s + 1) * channels] = (
            x_ref[s, :channels, :].astype(F32).T.astype(BF16)
        )
        turned = x_ref[s, channels:, :].astype(F32).T.astype(BF16)
        gout_ref[:, s * channels : s * channels + half] = turned[:64]
        gout_ref[:, s * channels + half : (s + 1) * channels] = turned[64:]


def local(tokens, dilations, taps, w_query, w_keyval, w_out, exponents, pair, w_bias, cotangent):
    count = lax.axis_size("seq")
    me = lax.axis_index("seq")
    rows, width = tokens.shape
    ch = width // count
    length = rows * count
    place = me.astype(jnp.int32).reshape(1)
    blocks = (count, ch, rows)

    turned_shape = (count, 2 * ch, rows)
    (first,) = call(
        flip_body,
        [(turned_shape, BF16)],
        "flip",
        0,
        4 * rows * width,
        scratch=[
            pltpu.VMEM((rows, width), BF16),
            pltpu.VMEM((rows, width), BF16),
            pltpu.VMEM(turned_shape, BF16),
            pltpu.SemaphoreType.DMA((count + 2,)),
        ],
        limit=63,
        space=ANY,
    )(tokens, cotangent)
    turned = exchange(first)
    (grad_attn,) = call(
        early_body, [((576, 128), BF16)], "early", 2 * rows * width * 512, 4 * MIB
    )(exponents, cotangent, w_out, pair, w_bias.T)
    my_taps = jnp.transpose(taps, (1, 0, 2))
    turn = pltpu.VMEM((256, 16), F32)
    across = [(i, (i + 4) % 8) for i in range(8)]
    around = {o: [(i, i // 4 * 4 + (i + o) % 4) for i in range(8)] for o in (1, 2, 3)}
    columns = [grad_attn] + [lax.ppermute(grad_attn, "seq", around[o]) for o in (1, 3, 2)]

    other = [lax.ppermute(grad_attn, "seq", across)]

    trunk_turned, slopes = call(
        conv_body,
        [(blocks, BF16), ((2, *blocks), BF16)],
        "conv",
        100 * length * ch,
        4 * MIB,
        scratch=[turn],
        limit=CONV_LIMIT,
    )(dilations, place, after(turned, grad_attn), my_taps)
    back = exchange(after(trunk_turned, *columns, *other))
    other += [lax.ppermute(c, "seq", across) for c in columns[1:3]]
    other += [lax.ppermute(other[0], "seq", around[2])]

    keyval, trunk = call(
        keyval_body,
        [((count, rows, 768), BF16), ((rows, width), BF16)],
        "keyval",
        2 * rows * width * 768,
        2 * MIB,
    )(exponents, back, w_keyval, w_query)
    keyval = exchange(after(keyval, *other))
    columns = columns + other
    (pack,) = call(
        query_body,
        [((count, 1040, 128), BF16)],
        "query",
        2 * rows * width * 512,
        3 * MIB,
        scratch=[pltpu.VMEM((count, 64, 128), BF16)],
    )(place, *columns)

    heads = (count, 512, 128)
    attended, grad_q, grad_kv = call(
        attention_body,
        [(heads, BF16), (heads, BF16), ((count, rows, 256), BF16)],
        "attention",
        12 * length * length * 512,
        8 * MIB,
        scratch=[
            pltpu.VMEM((length, 256), F32),
            pltpu.VMEM((length, 256), BF16),
            pltpu.VMEM((length, 128), BF16),
            pltpu.VMEM((128, length), BF16),
            pltpu.VMEM((128, length), BF16),
            pltpu.VMEM((count, 512, 256), BF16),
            pltpu.VMEM((2, length, 512), F32),
            pltpu.VMEM((2, length, 512), F32),
            pltpu.VMEM((2, length, 512), BF16),
            pltpu.VMEM((2, length, 512), BF16),
        ],
        limit=32,
    )(keyval, pack)

    (final,) = call(
        back_body,
        [((count, ch + ch // 2, rows), BF16)],
        "back",
        2 * length * ch * 1280,
        8 * MIB,
        scratch=[pltpu.VMEM(blocks, F32), turn],
    )(dilations, place, turned, attended, grad_q, grad_kv, w_query, w_keyval, my_taps, slopes)
    final = exchange(final)
    grad_query, grad_keyval = call(
        weights_body,
        [((ch, 512), BF16), ((ch, 256), BF16)],
        "weights",
        2 * length * ch * 768,
        4 * MIB,
    )(trunk_turned, grad_q, grad_kv)
    (output,) = call(output_body, [((rows, width), BF16)], "output", 2 * rows * width * 512, 3 * MIB)(
        place, trunk, attended, w_out
    )
    grad_tokens, grad_out = call(
        last_body, [((rows, width), BF16), ((64, width), BF16)], "last", 0, 2 * MIB
    )(final)
    return output, grad_tokens, grad_query, grad_keyval, grad_out


def solution(mesh):
    both = P(("dp", "seq"))
    in_specs = (both, P(), P(), P(), P(), P(), both, both, P(), both)
    return jax.shard_map(
        local, mesh=mesh, in_specs=in_specs, out_specs=(both,) * 5, check_vma=False
    )
```

profile of v0, /device:TPU:160, one launch (start us, length us, event | category | flops | bytes accessed | tf_op | source)
XLA Modules:
  0.0 108.7 jit_solution(14563186813730576106)
XLA Ops:
  0.6 2.5 %flip.1 = bf16[8,384,128]{2,1,0:T(8,128)(2,1)} custom-call(bf16[128,1536]{1,0:T(8,128)(2,1)} %tok_hbm.1, bf16[128,1536]{1,0:T(8,128)(2,1)} %cot_ref.1), custom_call_target="tpu_custom_call" | custom-call | bytes 786432 | tf_op jit(solution)/shard_map/flip/pallas_call | solution.py:30
  3.2 0.0 copy-start.4
  3.2 5.5 %all-to-all-start = ((bf16[8,384,128]{2,1,0:T(8,128)(2,1)}), bf16[8,384,128]{2,1,0:T(8,128)(2,1)S(1)}, u32[]{:S(2)}, u32[]{:S(2)}) async-start(bf16[8,384,128]{2,1,0:T(8,128)(2,1)} %flip.1), calls=%async_computation | async-start | bytes 1572864 | tf_op jit(solution)/shard_map/all_to_all | solution.py:45
  9.4 0.0 copy-start.16
  9.4 1.0 copy-done.16
  10.4 0.9 copy-done.21
  11.3 1.1 early.1.refs_0_
  12.4 2.1 %collective-permute-start.3 = (bf16[576,128]{1,0:T(8,128)(2,1)S(1)}, bf16[576,128]{1,0:T(8,128)(2,1)}, u32[]{:S(2)}, u32[]{:S(2)}) collective-permute-start(bf16[576,128]{1,0:T(8,128)(2,1)S(1)} %early.1.refs_0_), channel_id=1, source_target_pairs={{0,128},{32,160},{64,192},{96,224},{128,0},{160,32},{192,64},{224,... | collective-permute-start | bytes 442376 | tf_op jit(solution)/shard_map/ppermute | solution.py:415
  14.5 3.0 %collective-permute-start.2 = (bf16[576,128]{1,0:T(8,128)(2,1)S(1)}, bf16[576,128]{1,0:T(8,128)(2,1)}, u32[]{:S(2)}, u32[]{:S(2)}) collective-permute-start(bf16[576,128]{1,0:T(8,128)(2,1)S(1)} %early.1.refs_0_), channel_id=1, source_target_pairs={{0,64},{32,96},{64,0},{96,32},{128,192},{160,224},{192,128},{224,1... | collective-permute-start | bytes 442376 | tf_op jit(solution)/shard_map/ppermute | solution.py:413
  17.5 1.2 %collective-permute-start.1 = (bf16[576,128]{1,0:T(8,128)(2,1)S(1)}, bf16[576,128]{1,0:T(8,128)(2,1)}, u32[]{:S(2)}, u32[]{:S(2)}) collective-permute-start(bf16[576,128]{1,0:T(8,128)(2,1)S(1)} %early.1.refs_0_), channel_id=1, source_target_pairs={{0,96},{32,0},{64,32},{96,64},{128,224},{160,128},{192,160},{224,1... | collective-permute-start | bytes 442376 | tf_op jit(solution)/shard_map/ppermute | solution.py:413
  18.6 0.9 collective-permute-start
  19.5 2.6 %all-to-all-done.x_ref = bf16[8,384,128]{2,1,0:T(8,128)(2,1)S(1)} async-done(((bf16[8,384,128]{2,1,0:T(8,128)(2,1)}), bf16[8,384,128]{2,1,0:T(8,128)(2,1)S(1)}, u32[]{:S(2)}, u32[]{:S(2)}) %all-to-all-start) | async-done | bytes 786464 | tf_op jit(solution)/shard_map/all_to_all | solution.py:45
  22.1 0.9 copy-done
  23.0 5.5 %conv.1 = (bf16[8,192,128]{2,1,0:T(8,128)(2,1)}, bf16[2,8,192,128]{3,2,1,0:T(8,128)(2,1)}) custom-call(s32[2]{0:T(128)} %dil_ref.3, s32[1]{0:T(128)} %bitcast.me_ref, bf16[8,384,128]{2,1,0:T(8,128)(2,1)} %copy-done, f32[3,2,1536]{2,1,0:T(2,128)} %bitcast.3), custom_call_target="tpu_custom_call" | custom-call | flops 19660800 | bytes 4194304 | tf_op jit(solution)/shard_map/conv/pallas_call | solution.py:30
  28.5 0.0 collective-permute-done.3.refs_4_
  28.5 0.0 collective-permute-done.2.refs_3_
  28.5 0.0 collective-permute-done.1.refs_2_
  28.5 0.0 collective-permute-done.refs_1_
  28.5 3.9 %all-to-all-start.1 = ((bf16[8,192,128]{2,1,0:T(8,128)(2,1)}), bf16[8,192,128]{2,1,0:T(8,128)(2,1)S(1)}, u32[]{:S(2)}, u32[]{:S(2)}) async-start(bf16[8,192,128]{2,1,0:T(8,128)(2,1)} %get-tuple-element.21.x_ref), calls=%async_computation.1 | async-start | bytes 786432 | tf_op jit(solution)/shard_map/all_to_all | solution.py:45
  32.4 3.5 %collective-permute-start.6 = (bf16[576,128]{1,0:T(8,128)(2,1)}, bf16[576,128]{1,0:T(8,128)(2,1)S(1)}, u32[]{:S(2)}, u32[]{:S(2)}) collective-permute-start(bf16[576,128]{1,0:T(8,128)(2,1)} %collective-permute-done.3.refs_4_), channel_id=1, source_target_pairs={{0,64},{32,96},{64,0},{96,32},{128,192},{160,224},{192,128},{224,1... | collective-permute-start | bytes 442376 | tf_op jit(solution)/shard_map/ppermute | solution.py:428
  36.0 1.5 %collective-permute-start.5 = (bf16[576,128]{1,0:T(8,128)(2,1)}, bf16[576,128]{1,0:T(8,128)(2,1)S(1)}, u32[]{:S(2)}, u32[]{:S(2)}) collective-permute-start(bf16[576,128]{1,0:T(8,128)(2,1)} %collective-permute-done.1.refs_2_), channel_id=1, source_target_pairs={{0,128},{32,160},{64,192},{96,224},{128,0},{160,32},{192,64},{224,... | collective-permute-start | bytes 442376 | tf_op jit(solution)/shard_map/ppermute | solution.py:427
  37.4 0.6 collective-permute-start.4
  38.0 3.7 %all-to-all-done.1.x_ref = bf16[8,192,128]{2,1,0:T(8,128)(2,1)S(1)} async-done(((bf16[8,192,128]{2,1,0:T(8,128)(2,1)}), bf16[8,192,128]{2,1,0:T(8,128)(2,1)S(1)}, u32[]{:S(2)}, u32[]{:S(2)}) %all-to-all-start.1) | async-done | bytes 393248 | tf_op jit(solution)/shard_map/all_to_all | solution.py:45
  41.7 1.4 %copy-done.2 = bf16[1536,512]{1,0:T(8,128)(2,1)S(1)} copy-done((bf16[1536,512]{1,0:T(8,128)(2,1)S(1)}, bf16[1536,512]{1,0:T(8,128)(2,1)}, u32[]{:S(2)}) %copy-start.2) | copy-done | bytes 1572888
  43.1 1.1 %copy-done.8 = bf16[1536,256]{1,0:T(8,128)(2,1)S(1)} copy-done((bf16[1536,256]{1,0:T(8,128)(2,1)S(1)}, bf16[1536,256]{1,0:T(8,128)(2,1)}, u32[]{:S(2)}) %copy-start.8) | copy-done | bytes 786456
  44.2 2.0 %keyval.1 = (bf16[8,128,768]{2,1,0:T(8,128)(2,1)}, bf16[128,1536]{1,0:T(8,128)(2,1)S(1)}) custom-call(s32[1]{0:T(128)S(6)} %copy.15.exp_ref, bf16[8,192,128]{2,1,0:T(8,128)(2,1)S(1)} %all-to-all-done.1.x_ref, bf16[1536,256]{1,0:T(8,128)(2,1)S(1)} %copy-done.8, bf16[1536,512]{1,0:T(8,128)(2,1)S(1)} %copy-done.2), custom_call_target="tpu_custom_call" | custom-call | flops 301989888 | bytes 2097152 | tf_op jit(solution)/shard_map/keyval/pallas_call | solution.py:30
  46.2 0.0 collective-permute-done.6.refs_7_
  46.2 0.0 collective-permute-done.5.refs_6_
  46.2 0.0 collective-permute-done.4.refs_5_
  46.2 0.7 copy-done.18
  46.9 4.5 %all-to-all-start.2 = ((bf16[8,128,768]{2,1,0:T(8,128)(2,1)}), bf16[8,128,768]{2,1,0:T(8,128)(2,1)}, u32[]{:S(2)}, u32[]{:S(2)}) async-start(bf16[8,128,768]{2,1,0:T(8,128)(2,1)} %get-tuple-element.24), calls=%async_computation.2 | async-start | bytes 3145728 | tf_op jit(solution)/shard_map/all_to_all | solution.py:45
  51.4 1.8 %query.1.pack_ref = bf16[8,1040,128]{2,1,0:T(8,128)(2,1)S(1)} custom-call(s32[1]{0:T(128)} %bitcast.me_ref, bf16[576,128]{1,0:T(8,128)(2,1)S(1)} %early.1.refs_0_, bf16[576,128]{1,0:T(8,128)(2,1)} %collective-permute-done.refs_1_, bf16[576,128]{1,0:T(8,128)(2,1)} %collective-permute-done.1.refs_2_, bf16[576,128]{1,0:T(8,128)(2,1)} %collective-permute-done.2.refs_3_, ...), custom_call_target="tpu_custom_call" | custom-call | flops 201326592 | bytes 3145728 | tf_op jit(solution)/shard_map/query/pallas_call | solution.py:30
  53.2 1.4 %copy-done.11 = bf16[8,1040,128]{2,1,0:T(8,128)(2,1)} copy-done((bf16[8,1040,128]{2,1,0:T(8,128)(2,1)}, bf16[8,1040,128]{2,1,0:T(8,128)(2,1)S(1)}, u32[]{:S(2)}) %copy-start.11) | copy-done | bytes 2129944
  54.5 13.6 %all-to-all-done.2.kv_ref = bf16[8,128,768]{2,1,0:T(8,128)(2,1)} async-done(((bf16[8,128,768]{2,1,0:T(8,128)(2,1)}), bf16[8,128,768]{2,1,0:T(8,128)(2,1)}, u32[]{:S(2)}, u32[]{:S(2)}) %all-to-all-start.2) | async-done | bytes 1572896 | tf_op jit(solution)/shard_map/all_to_all | solution.py:45
  68.2 1.6 %copy-done.12 = bf16[8,1040,128]{2,1,0:T(8,128)(2,1)S(1)} copy-done((bf16[8,1040,128]{2,1,0:T(8,128)(2,1)S(1)}, bf16[8,1040,128]{2,1,0:T(8,128)(2,1)}, u32[]{:S(2)}) %copy-start.12) | copy-done | bytes 2129944
  69.8 17.3 %attention.1 = (bf16[8,512,128]{2,1,0:T(8,128)(2,1)S(1)}, bf16[8,512,128]{2,1,0:T(8,128)(2,1)S(1)}, bf16[8,128,256]{2,1,0:T(8,128)(2,1)S(1)}) custom-call(bf16[8,128,768]{2,1,0:T(8,128)(2,1)} %all-to-all-done.2.kv_ref, bf16[8,1040,128]{2,1,0:T(8,128)(2,1)S(1)} %copy-done.12), custom_call_target="tpu_custom_call" | custom-call | flops 6442450944 | bytes 8388608 | tf_op jit(solution)/shard_map/attention/pallas_call | solution.py:30
  87.2 4.2 %back.1 = bf16[8,288,128]{2,1,0:T(8,128)(2,1)S(1)} custom-call(s32[2]{0:T(128)S(1)} %copy-done.22, s32[1]{0:T(128)} %bitcast.me_ref, bf16[8,384,128]{2,1,0:T(8,128)(2,1)S(1)} %copy-done.1, bf16[8,512,128]{2,1,0:T(8,128)(2,1)S(1)} %get-tuple-element.25.att_ref, bf16[8,512,128]{2,1,0:T(8,128)(2,1)S(1)} %get-tuple-element.26.gq_ref, ...), custom_call_target="tpu_custom_call" | custom-call | flops 503316480 | bytes 8388608 | tf_op jit(solution)/shard_map/back/pallas_call | solution.py:30
  91.4 1.0 copy-done.6
  92.4 0.8 copy-done.10
  93.2 0.8 copy-done.13
  94.0 3.6 %all-to-all-start.3 = ((bf16[8,288,128]{2,1,0:T(8,128)(2,1)}), bf16[8,288,128]{2,1,0:T(8,128)(2,1)S(1)}, u32[]{:S(2)}, u32[]{:S(2)}) async-start(bf16[8,288,128]{2,1,0:T(8,128)(2,1)} %copy-done.10), calls=%async_computation.3 | async-start | bytes 1179648 | tf_op jit(solution)/shard_map/all_to_all | solution.py:45
  97.7 1.4 %copy-done.5 = bf16[512,1536]{1,0:T(8,128)(2,1)S(1)} copy-done((bf16[512,1536]{1,0:T(8,128)(2,1)S(1)}, bf16[512,1536]{1,0:T(8,128)(2,1)}, u32[]{:S(2)}) %copy-start.5) | copy-done | bytes 1572888
  99.1 1.0 copy-done.19
  100.1 1.4 %output.1 = bf16[128,1536]{1,0:T(8,128)(2,1)} custom-call(s32[1]{0:T(128)} %bitcast.me_ref, bf16[128,1536]{1,0:T(8,128)(2,1)S(1)} %copy-done.19, bf16[8,512,128]{2,1,0:T(8,128)(2,1)S(1)} %get-tuple-element.25.att_ref, bf16[512,1536]{1,0:T(8,128)(2,1)S(1)} %copy-done.5), custom_call_target="tpu_custom_call" | custom-call | flops 201326592 | bytes 3145728 | tf_op jit(solution)/shard_map/output/pallas_call | solution.py:30
  101.4 0.1 copy-done.15
  101.5 1.5 %weights.1 = (bf16[192,512]{1,0:T(8,128)(2,1)}, bf16[192,256]{1,0:T(8,128)(2,1)}) custom-call(bf16[8,192,128]{2,1,0:T(8,128)(2,1)S(1)} %copy-done.15, bf16[8,512,128]{2,1,0:T(8,128)(2,1)S(1)} %copy-done.7, bf16[8,128,256]{2,1,0:T(8,128)(2,1)S(1)} %copy-done.14), custom_call_target="tpu_custom_call" | custom-call | flops 301989888 | bytes 4194304 | tf_op jit(solution)/shard_map/weights/pallas_call | solution.py:30
  103.0 4.5 %all-to-all-done.3.x_ref = bf16[8,288,128]{2,1,0:T(8,128)(2,1)S(1)} async-done(((bf16[8,288,128]{2,1,0:T(8,128)(2,1)}), bf16[8,288,128]{2,1,0:T(8,128)(2,1)S(1)}, u32[]{:S(2)}, u32[]{:S(2)}) %all-to-all-start.3) | async-done | bytes 589856 | tf_op jit(solution)/shard_map/all_to_all | solution.py:45
  107.5 1.3 %last.1 = (bf16[128,1536]{1,0:T(8,128)(2,1)}, bf16[64,1536]{1,0:T(8,128)(2,1)}) custom-call(bf16[8,288,128]{2,1,0:T(8,128)(2,1)S(1)} %all-to-all-done.3.x_ref), custom_call_target="tpu_custom_call" | custom-call | bytes 2097152 | tf_op jit(solution)/shard_map/last/pallas_call | solution.py:30
  (32 shorter events, 0.1 us)
Async XLA Ops:
  0.6 8.7 %copy-start.23 = (f32[128,4]{0,1:T(4,128)S(1)}, f32[128,4]{0,1:T(4,128)}, u32[]{:S(2)}) copy-start(f32[128,4]{0,1:T(4,128)} %param.18) | copy-start | bytes 6148
  3.2 6.2 %copy-start.4 = (bf16[512,1536]{1,0:T(8,128)(2,1)S(1)}, bf16[512,1536]{1,0:T(8,128)(2,1)}, u32[]{:S(2)}) copy-start(bf16[512,1536]{1,0:T(8,128)(2,1)} %wout_ref.3) | copy-start | bytes 4718596
  3.2 18.9 %all-to-all-start = ((bf16[8,384,128]{2,1,0:T(8,128)(2,1)}), bf16[8,384,128]{2,1,0:T(8,128)(2,1)S(1)}, u32[]{:S(2)}, u32[]{:S(2)}) async-start(bf16[8,384,128]{2,1,0:T(8,128)(2,1)} %flip.1), calls=%async_computation | async-start | bytes 1572864 | tf_op jit(solution)/shard_map/all_to_all | solution.py:45
  9.4 1.0 copy-start.16
  10.4 0.9 copy-start.21
  12.4 16.1 %collective-permute-start.3 = (bf16[576,128]{1,0:T(8,128)(2,1)S(1)}, bf16[576,128]{1,0:T(8,128)(2,1)}, u32[]{:S(2)}, u32[]{:S(2)}) collective-permute-start(bf16[576,128]{1,0:T(8,128)(2,1)S(1)} %early.1.refs_0_), channel_id=1, source_target_pairs={{0,128},{32,160},{64,192},{96,224},{128,0},{160,32},{192,64},{224,... | collective-permute-start | bytes 442376 | tf_op jit(solution)/shard_map/ppermute | solution.py:415
  14.5 14.0 %collective-permute-start.2 = (bf16[576,128]{1,0:T(8,128)(2,1)S(1)}, bf16[576,128]{1,0:T(8,128)(2,1)}, u32[]{:S(2)}, u32[]{:S(2)}) collective-permute-start(bf16[576,128]{1,0:T(8,128)(2,1)S(1)} %early.1.refs_0_), channel_id=1, source_target_pairs={{0,64},{32,96},{64,0},{96,32},{128,192},{160,224},{192,128},{224,1... | collective-permute-start | bytes 442376 | tf_op jit(solution)/shard_map/ppermute | solution.py:413
  17.5 11.0 %collective-permute-start.1 = (bf16[576,128]{1,0:T(8,128)(2,1)S(1)}, bf16[576,128]{1,0:T(8,128)(2,1)}, u32[]{:S(2)}, u32[]{:S(2)}) collective-permute-start(bf16[576,128]{1,0:T(8,128)(2,1)S(1)} %early.1.refs_0_), channel_id=1, source_target_pairs={{0,96},{32,0},{64,32},{96,64},{128,224},{160,128},{192,160},{224,1... | collective-permute-start | bytes 442376 | tf_op jit(solution)/shard_map/ppermute | solution.py:413
  18.6 9.9 %collective-permute-start = (bf16[576,128]{1,0:T(8,128)(2,1)S(1)}, bf16[576,128]{1,0:T(8,128)(2,1)}, u32[]{:S(2)}, u32[]{:S(2)}) collective-permute-start(bf16[576,128]{1,0:T(8,128)(2,1)S(1)} %early.1.refs_0_), channel_id=1, source_target_pairs={{0,32},{32,64},{64,96},{96,0},{128,160},{160,192},{192,224},{224,1... | collective-permute-start | bytes 442376 | tf_op jit(solution)/shard_map/ppermute | solution.py:413
  22.1 0.9 copy-start
  28.5 13.2 %all-to-all-start.1 = ((bf16[8,192,128]{2,1,0:T(8,128)(2,1)}), bf16[8,192,128]{2,1,0:T(8,128)(2,1)S(1)}, u32[]{:S(2)}, u32[]{:S(2)}) async-start(bf16[8,192,128]{2,1,0:T(8,128)(2,1)} %get-tuple-element.21.x_ref), calls=%async_computation.1 | async-start | bytes 786432 | tf_op jit(solution)/shard_map/all_to_all | solution.py:45
  32.4 13.8 %collective-permute-start.6 = (bf16[576,128]{1,0:T(8,128)(2,1)}, bf16[576,128]{1,0:T(8,128)(2,1)S(1)}, u32[]{:S(2)}, u32[]{:S(2)}) collective-permute-start(bf16[576,128]{1,0:T(8,128)(2,1)} %collective-permute-done.3.refs_4_), channel_id=1, source_target_pairs={{0,64},{32,96},{64,0},{96,32},{128,192},{160,224},{192,128},{224,1... | collective-permute-start | bytes 442376 | tf_op jit(solution)/shard_map/ppermute | solution.py:428
  36.0 10.2 %collective-permute-start.5 = (bf16[576,128]{1,0:T(8,128)(2,1)}, bf16[576,128]{1,0:T(8,128)(2,1)S(1)}, u32[]{:S(2)}, u32[]{:S(2)}) collective-permute-start(bf16[576,128]{1,0:T(8,128)(2,1)} %collective-permute-done.1.refs_2_), channel_id=1, source_target_pairs={{0,128},{32,160},{64,192},{96,224},{128,0},{160,32},{192,64},{224,... | collective-permute-start | bytes 442376 | tf_op jit(solution)/shard_map/ppermute | solution.py:427
  37.4 8.8 %collective-permute-start.4 = (bf16[576,128]{1,0:T(8,128)(2,1)}, bf16[576,128]{1,0:T(8,128)(2,1)S(1)}, u32[]{:S(2)}, u32[]{:S(2)}) collective-permute-start(bf16[576,128]{1,0:T(8,128)(2,1)} %collective-permute-done.refs_1_), channel_id=1, source_target_pairs={{0,128},{32,160},{64,192},{96,224},{128,0},{160,32},{192,64},{224,... | collective-permute-start | bytes 442376 | tf_op jit(solution)/shard_map/ppermute | solution.py:427
  41.7 1.4 %copy-start.2 = (bf16[1536,512]{1,0:T(8,128)(2,1)S(1)}, bf16[1536,512]{1,0:T(8,128)(2,1)}, u32[]{:S(2)}) copy-start(bf16[1536,512]{1,0:T(8,128)(2,1)} %wq_ref.3) | copy-start | bytes 4718596
  43.1 1.1 %copy-start.8 = (bf16[1536,256]{1,0:T(8,128)(2,1)S(1)}, bf16[1536,256]{1,0:T(8,128)(2,1)}, u32[]{:S(2)}) copy-start(bf16[1536,256]{1,0:T(8,128)(2,1)} %wkv_ref.3) | copy-start | bytes 2359300
  46.2 0.7 copy-start.18
  46.9 21.3 %all-to-all-start.2 = ((bf16[8,128,768]{2,1,0:T(8,128)(2,1)}), bf16[8,128,768]{2,1,0:T(8,128)(2,1)}, u32[]{:S(2)}, u32[]{:S(2)}) async-start(bf16[8,128,768]{2,1,0:T(8,128)(2,1)} %get-tuple-element.24), calls=%async_computation.2 | async-start | bytes 3145728 | tf_op jit(solution)/shard_map/all_to_all | solution.py:45
  53.2 1.4 %copy-start.11 = (bf16[8,1040,128]{2,1,0:T(8,128)(2,1)}, bf16[8,1040,128]{2,1,0:T(8,128)(2,1)S(1)}, u32[]{:S(2)}) copy-start(bf16[8,1040,128]{2,1,0:T(8,128)(2,1)S(1)} %query.1.pack_ref) | copy-start | bytes 6389764
  54.5 32.6 %copy-start.1 = (bf16[8,384,128]{2,1,0:T(8,128)(2,1)S(1)}, bf16[8,384,128]{2,1,0:T(8,128)(2,1)}, u32[]{:S(2)}) copy-start(bf16[8,384,128]{2,1,0:T(8,128)(2,1)} %copy-done) | copy-start | bytes 2359300
  54.5 32.6 %copy-start.3 = (bf16[1536,512]{1,0:T(8,128)(2,1)S(1)}, bf16[1536,512]{1,0:T(8,128)(2,1)}, u32[]{:S(2)}) copy-start(bf16[1536,512]{1,0:T(8,128)(2,1)} %wq_ref.3) | copy-start | bytes 4718596
  68.2 1.6 %copy-start.12 = (bf16[8,1040,128]{2,1,0:T(8,128)(2,1)S(1)}, bf16[8,1040,128]{2,1,0:T(8,128)(2,1)}, u32[]{:S(2)}) copy-start(bf16[8,1040,128]{2,1,0:T(8,128)(2,1)} %copy-done.11) | copy-start | bytes 6389764
  69.8 17.3 %copy-start.9 = (bf16[1536,256]{1,0:T(8,128)(2,1)S(1)}, bf16[1536,256]{1,0:T(8,128)(2,1)}, u32[]{:S(2)}) copy-start(bf16[1536,256]{1,0:T(8,128)(2,1)} %wkv_ref.3) | copy-start | bytes 2359300
  69.8 17.3 %copy-start.17 = (bf16[2,8,192,128]{3,2,1,0:T(8,128)(2,1)S(1)}, bf16[2,8,192,128]{3,2,1,0:T(8,128)(2,1)}, u32[]{:S(2)}) copy-start(bf16[2,8,192,128]{3,2,1,0:T(8,128)(2,1)} %get-tuple-element.28.slope_ref) | copy-start | bytes 2359300
  69.8 17.3 %copy-start.20 = (f32[2,3,1536]{2,0,1:T(2,128)S(1)}, f32[2,3,1536]{2,0,1:T(2,128)}, u32[]{:S(2)}) copy-start(f32[2,3,1536]{2,0,1:T(2,128)} %param.12) | copy-start | bytes 110596
  69.8 17.3 %copy-start.22 = (s32[2]{0:T(128)S(1)}, s32[2]{0:T(128)}, u32[]{:S(2)}) copy-start(s32[2]{0:T(128)} %dil_ref.3) | copy-start | bytes 28
  91.4 1.0 copy-start.6
  92.4 0.8 copy-start.10
  93.2 0.8 copy-start.13
  94.0 13.4 %all-to-all-start.3 = ((bf16[8,288,128]{2,1,0:T(8,128)(2,1)}), bf16[8,288,128]{2,1,0:T(8,128)(2,1)S(1)}, u32[]{:S(2)}, u32[]{:S(2)}) async-start(bf16[8,288,128]{2,1,0:T(8,128)(2,1)} %copy-done.10), calls=%async_computation.3 | async-start | bytes 1179648 | tf_op jit(solution)/shard_map/all_to_all | solution.py:45
  97.7 1.4 %copy-start.5 = (bf16[512,1536]{1,0:T(8,128)(2,1)S(1)}, bf16[512,1536]{1,0:T(8,128)(2,1)}, u32[]{:S(2)}) copy-start(bf16[512,1536]{1,0:T(8,128)(2,1)} %wout_ref.3) | copy-start | bytes 4718596
  99.1 1.0 copy-start.19
  100.1 1.4 %copy-start.7 = (bf16[8,512,128]{2,1,0:T(8,128)(2,1)S(1)}, bf16[8,512,128]{2,1,0:T(8,128)(2,1)}, u32[]{:S(2)}) copy-start(bf16[8,512,128]{2,1,0:T(8,128)(2,1)} %copy-done.6) | copy-start | bytes 3145732
  100.1 1.4 %copy-start.14 = (bf16[8,128,256]{2,1,0:T(8,128)(2,1)S(1)}, bf16[8,128,256]{2,1,0:T(8,128)(2,1)}, u32[]{:S(2)}) copy-start(bf16[8,128,256]{2,1,0:T(8,128)(2,1)} %copy-done.13) | copy-start | bytes 1572868
  100.1 1.5 %copy-start.15 = (bf16[8,192,128]{2,1,0:T(8,128)(2,1)S(1)}, bf16[8,192,128]{2,1,0:T(8,128)(2,1)}, u32[]{:S(2)}) copy-start(bf16[8,192,128]{2,1,0:T(8,128)(2,1)} %get-tuple-element.21.x_ref) | copy-start | bytes 1179652
where the time goes:
time: 109 us
  Pallas kernels  38.4 us (35%)
  starting transfers between devices  30.2 us (28%)
  waiting for transfers between devices  24.5 us (22%)
  local copies, waits for them, and re-layouts  14.2 us (13%)
  between operations  1.5 us (1%)
    pallas_call x10, Pallas kernels, run(): pl.pallas_call(body, out_shape=[jax.ShapeDtypeStruct(s, d) for s, d in ou...  38.4 us
    all_to_all x4, waiting for transfers between devices, exchange(): return lax.all_to_all(x, 'seq', split_axis=0, concat_axis=0, tiled=True)  24.4 us
    all_to_all x4, starting transfers between devices, exchange(): return lax.all_to_all(x, 'seq', split_axis=0, concat_axis=0, tiled=True)  17.5 us
    unnamed x48, local copies, waits for them, and re-layouts  14.2 us
    ppermute x3, starting transfers between devices, local(): lax.ppermute(grad_attn, 'seq', around[o])  4.99 us
    ppermute x1, starting transfers between devices, local(): other += [lax.ppermute(other[0], 'seq', around[2])]  3.53 us
  transfers between devices with their start and end apart: 11, of which 4 were waited for; matrix products, arithmetic and copies ran while one was open for 0% of the time, Pallas kernels for 12%

commit v1 on v0

--- a/solution.py
+++ b/solution.py
@@ -168,21 +168,35 @@
     return jnp.where(e >= 0, up, down), jnp.where(e >= 0, down, up)
 
 
-def keyval_body(exp_ref, x_ref, wkv_ref, wq_ref, send_ref, trunk_ref):
+def keyval_body(
+    exp_ref, x_hbm, wkv_hbm, wq_hbm, send_hbm, trunk_hbm,
+    x_ref, wkv_ref, wq_ref, send_ref, trunk_ref, sems,
+):
+    pairs = ((x_hbm, x_ref), (wkv_hbm, wkv_ref), (wq_hbm, wq_ref))
+    reads = [pltpu.make_async_copy(a, b, sems.at[k]) for k, (a, b) in enumerate(pairs)]
+    for copy in reads:
+        copy.start()
+    reads[0].wait()
     count, channels, _ = x_ref.shape
     for s in range(count):
         trunk_ref[:, s * channels : (s + 1) * channels] = x_ref[s].astype(F32).T.astype(BF16)
+    writes = [pltpu.make_async_copy(trunk_ref, trunk_hbm, sems.at[3])]
+    writes[0].start()
     factor, inverse = power_of_two(exp_ref[0])
+    reads[1].wait()
     unscaled = nn(trunk_ref[...], wkv_ref[...]) * inverse
     codes = jnp.clip(unscaled, -CLIP_LEVEL, CLIP_LEVEL).astype(BF16).astype(F32)
     marked = jnp.where(
         jnp.abs(unscaled) < CLIP_LEVEL, codes, jnp.where(unscaled > 0.0, F32(512.0), F32(-512.0))
     )
-    marked = (marked * factor).astype(BF16)
-    query = nn(trunk_ref[...], wq_ref[...]).astype(BF16)
-    for s in range(count):
-        send_ref[s, :, :256] = marked
-        send_ref[s, :, 256:] = query
+    send_ref[:, :256] = (marked * factor).astype(BF16)
+    reads[2].wait()
+    send_ref[:, 256:] = nn(trunk_ref[...], wq_ref[...]).astype(BF16)
+    for s in range(count):
+        writes.append(pltpu.make_async_copy(send_ref, send_hbm.at[s], sems.at[4 + s]))
+        writes[-1].start()
+    for copy in writes:
+        copy.wait()
 
 
 def query_body(me_ref, *refs):
@@ -433,6 +447,16 @@
         "keyval",
         2 * rows * width * 768,
         2 * MIB,
+        scratch=[
+            pltpu.VMEM(blocks, BF16),
+            pltpu.VMEM((width, 256), BF16),
+            pltpu.VMEM((width, 512), BF16),
+            pltpu.VMEM((rows, 768), BF16),
+            pltpu.VMEM((rows, width), BF16),
+            pltpu.SemaphoreType.DMA((4 + count,)),
+        ],
+        limit=63,
+        space=ANY,
     )(exponents, back, w_keyval, w_query)
     keyval = exchange(after(keyval, *other))
     columns = columns + other

time: 109 us -> 110 us (level)
  local copies, waits for them, and re-layouts: 14.2 us -> 11.6 us
  Pallas kernels: 38.4 us -> 39.9 us
  waiting for transfers between devices: 24.5 us -> 25.7 us
    unnamed x48 -> x44, local copies, waits for them, and re-layouts: 14.2 us -> 11.6 us
    pallas_call x10, Pallas kernels: 38.4 us -> 39.9 us  [run(): pl.pallas_call(body, out_shape=[jax.ShapeDtypeStruct(s, d) for s, d in ou...]
    all_to_all x4, waiting for transfers between devices: 24.4 us -> 25.7 us  [exchange(): return lax.all_to_all(x, 'seq', split_axis=0, concat_axis=0, tiled=True)]
  transfers between devices with their start and end apart: 11 -> 11, of which waited for: 4 -> 4; matrix products, arithmetic and copies ran while one was open for 0% -> 0% of each run, Pallas kernels for 12% -> 13%
where the time goes in v1:
time: 110 us; the launch traced here: 109 us
  Pallas kernels  39.9 us (36%)
  starting transfers between devices  30.2 us (27%)
  waiting for transfers between devices  25.7 us (23%)
  local copies, waits for them, and re-layouts  11.6 us (11%)
  between operations  1.51 us (1%)
    pallas_call x10, Pallas kernels, run(): pl.pallas_call(body, out_shape=[jax.ShapeDtypeStruct(s, d) for s, d in ou...  39.9 us
    all_to_all x4, waiting for transfers between devices, exchange(): return lax.all_to_all(x, 'seq', split_axis=0, concat_axis=0, tiled=True)  25.7 us
    all_to_all x4, starting transfers between devices, exchange(): return lax.all_to_all(x, 'seq', split_axis=0, concat_axis=0, tiled=True)  17.6 us
    unnamed x44, local copies, waits for them, and re-layouts  11.6 us
    ppermute x3, starting transfers between devices, local(): lax.ppermute(grad_attn, 'seq', around[o])  4.99 us
    ppermute x1, starting transfers between devices, local(): other += [lax.ppermute(other[0], 'seq', around[2])]  3.53 us
  transfers between devices with their start and end apart: 11, of which 4 were waited for; matrix products, arithmetic and copies ran while one was open for 0% of the time, Pallas kernels for 13%

profile of v1, /device:TPU:160, one launch (start us, length us, event | category | flops | bytes accessed | tf_op | source)
XLA Modules:
  0.0 108.9 jit_solution(6305989894376617766)
XLA Ops:
  0.6 0.0 copy-start.20
  0.6 2.5 %flip.1 = bf16[8,384,128]{2,1,0:T(8,128)(2,1)} custom-call(bf16[128,1536]{1,0:T(8,128)(2,1)} %tok_hbm.1, bf16[128,1536]{1,0:T(8,128)(2,1)} %cot_ref.1), custom_call_target="tpu_custom_call" | custom-call | bytes 786432 | tf_op jit(solution)/shard_map/flip/pallas_call | solution.py:30
  3.1 0.0 copy-start.3
  3.2 5.5 %all-to-all-start = ((bf16[8,384,128]{2,1,0:T(8,128)(2,1)}), bf16[8,384,128]{2,1,0:T(8,128)(2,1)S(1)}, u32[]{:S(2)}, u32[]{:S(2)}) async-start(bf16[8,384,128]{2,1,0:T(8,128)(2,1)} %flip.1), calls=%async_computation | async-start | bytes 1572864 | tf_op jit(solution)/shard_map/all_to_all | solution.py:45
  9.4 0.0 copy-start.14
  9.4 1.0 copy-done.14
  10.4 0.9 copy-done.18
  11.3 1.1 early.1.refs_0_
  12.4 2.1 %collective-permute-start.3 = (bf16[576,128]{1,0:T(8,128)(2,1)S(1)}, bf16[576,128]{1,0:T(8,128)(2,1)}, u32[]{:S(2)}, u32[]{:S(2)}) collective-permute-start(bf16[576,128]{1,0:T(8,128)(2,1)S(1)} %early.1.refs_0_), channel_id=1, source_target_pairs={{0,128},{32,160},{64,192},{96,224},{128,0},{160,32},{192,64},{224,... | collective-permute-start | bytes 442376 | tf_op jit(solution)/shard_map/ppermute | solution.py:429
  14.5 3.0 %collective-permute-start.2 = (bf16[576,128]{1,0:T(8,128)(2,1)S(1)}, bf16[576,128]{1,0:T(8,128)(2,1)}, u32[]{:S(2)}, u32[]{:S(2)}) collective-permute-start(bf16[576,128]{1,0:T(8,128)(2,1)S(1)} %early.1.refs_0_), channel_id=1, source_target_pairs={{0,64},{32,96},{64,0},{96,32},{128,192},{160,224},{192,128},{224,1... | collective-permute-start | bytes 442376 | tf_op jit(solution)/shard_map/ppermute | solution.py:427
  17.5 1.2 %collective-permute-start.1 = (bf16[576,128]{1,0:T(8,128)(2,1)S(1)}, bf16[576,128]{1,0:T(8,128)(2,1)}, u32[]{:S(2)}, u32[]{:S(2)}) collective-permute-start(bf16[576,128]{1,0:T(8,128)(2,1)S(1)} %early.1.refs_0_), channel_id=1, source_target_pairs={{0,96},{32,0},{64,32},{96,64},{128,224},{160,128},{192,160},{224,1... | collective-permute-start | bytes 442376 | tf_op jit(solution)/shard_map/ppermute | solution.py:427
  18.6 0.9 collective-permute-start
  19.5 2.6 %all-to-all-done.x_ref = bf16[8,384,128]{2,1,0:T(8,128)(2,1)S(1)} async-done(((bf16[8,384,128]{2,1,0:T(8,128)(2,1)}), bf16[8,384,128]{2,1,0:T(8,128)(2,1)S(1)}, u32[]{:S(2)}, u32[]{:S(2)}) %all-to-all-start) | async-done | bytes 786464 | tf_op jit(solution)/shard_map/all_to_all | solution.py:45
  22.1 0.9 copy-done
  23.0 5.5 %conv.1 = (bf16[8,192,128]{2,1,0:T(8,128)(2,1)}, bf16[2,8,192,128]{3,2,1,0:T(8,128)(2,1)}) custom-call(s32[2]{0:T(128)} %dil_ref.3, s32[1]{0:T(128)} %bitcast.me_ref, bf16[8,384,128]{2,1,0:T(8,128)(2,1)} %copy-done, f32[3,2,1536]{2,1,0:T(2,128)} %bitcast.3), custom_call_target="tpu_custom_call" | custom-call | flops 19660800 | bytes 4194304 | tf_op jit(solution)/shard_map/conv/pallas_call | solution.py:30
  28.5 0.0 collective-permute-done.3.refs_4_
  28.5 0.0 collective-permute-done.2.refs_3_
  28.5 0.0 collective-permute-done.1.refs_2_
  28.5 0.0 collective-permute-done.refs_1_
  28.5 3.9 %all-to-all-start.1 = ((bf16[8,192,128]{2,1,0:T(8,128)(2,1)}), bf16[8,192,128]{2,1,0:T(8,128)(2,1)S(1)}, u32[]{:S(2)}, u32[]{:S(2)}) async-start(bf16[8,192,128]{2,1,0:T(8,128)(2,1)} %get-tuple-element.21.x_ref), calls=%async_computation.1 | async-start | bytes 786432 | tf_op jit(solution)/shard_map/all_to_all | solution.py:45
  32.4 3.5 %collective-permute-start.6 = (bf16[576,128]{1,0:T(8,128)(2,1)}, bf16[576,128]{1,0:T(8,128)(2,1)S(1)}, u32[]{:S(2)}, u32[]{:S(2)}) collective-permute-start(bf16[576,128]{1,0:T(8,128)(2,1)} %collective-permute-done.3.refs_4_), channel_id=1, source_target_pairs={{0,64},{32,96},{64,0},{96,32},{128,192},{160,224},{192,128},{224,1... | collective-permute-start | bytes 442376 | tf_op jit(solution)/shard_map/ppermute | solution.py:442
  35.9 1.5 %collective-permute-start.5 = (bf16[576,128]{1,0:T(8,128)(2,1)}, bf16[576,128]{1,0:T(8,128)(2,1)S(1)}, u32[]{:S(2)}, u32[]{:S(2)}) collective-permute-start(bf16[576,128]{1,0:T(8,128)(2,1)} %collective-permute-done.1.refs_2_), channel_id=1, source_target_pairs={{0,128},{32,160},{64,192},{96,224},{128,0},{160,32},{192,64},{224,... | collective-permute-start | bytes 442376 | tf_op jit(solution)/shard_map/ppermute | solution.py:441
  37.4 0.6 collective-permute-start.4
  38.0 3.7 %all-to-all-done.1.x_hbm = bf16[8,192,128]{2,1,0:T(8,128)(2,1)S(1)} async-done(((bf16[8,192,128]{2,1,0:T(8,128)(2,1)}), bf16[8,192,128]{2,1,0:T(8,128)(2,1)S(1)}, u32[]{:S(2)}, u32[]{:S(2)}) %all-to-all-start.1) | async-done | bytes 393248 | tf_op jit(solution)/shard_map/all_to_all | solution.py:45
  41.7 0.7 copy-done.21
  42.4 3.4 %keyval.1 = (bf16[8,128,768]{2,1,0:T(8,128)(2,1)}, bf16[128,1536]{1,0:T(8,128)(2,1)}) custom-call(s32[1]{0:T(128)S(6)} %copy.15.exp_ref, bf16[8,192,128]{2,1,0:T(8,128)(2,1)} %copy-done.21, bf16[1536,256]{1,0:T(8,128)(2,1)} %wkv_ref.1, bf16[1536,512]{1,0:T(8,128)(2,1)} %wq_ref.1), custom_call_target="tpu_custom_call" | custom-call | flops 301989888 | bytes 2097152 | tf_op jit(solution)/shard_map/keyval/pallas_call | solution.py:30
  45.8 0.0 collective-permute-done.6.refs_7_
  45.9 0.0 collective-permute-done.5.refs_6_
  45.9 0.0 collective-permute-done.4.refs_5_
  45.9 4.5 %all-to-all-start.2 = ((bf16[8,128,768]{2,1,0:T(8,128)(2,1)}), bf16[8,128,768]{2,1,0:T(8,128)(2,1)}, u32[]{:S(2)}, u32[]{:S(2)}) async-start(bf16[8,128,768]{2,1,0:T(8,128)(2,1)} %get-tuple-element.24), calls=%async_computation.2 | async-start | bytes 3145728 | tf_op jit(solution)/shard_map/all_to_all | solution.py:45
  50.4 1.8 %query.1.pack_ref = bf16[8,1040,128]{2,1,0:T(8,128)(2,1)S(1)} custom-call(s32[1]{0:T(128)} %bitcast.me_ref, bf16[576,128]{1,0:T(8,128)(2,1)S(1)} %early.1.refs_0_, bf16[576,128]{1,0:T(8,128)(2,1)} %collective-permute-done.refs_1_, bf16[576,128]{1,0:T(8,128)(2,1)} %collective-permute-done.1.refs_2_, bf16[576,128]{1,0:T(8,128)(2,1)} %collective-permute-done.2.refs_3_, ...), custom_call_target="tpu_custom_call" | custom-call | flops 201326592 | bytes 3145728 | tf_op jit(solution)/shard_map/query/pallas_call | solution.py:30
  52.1 0.0 copy-start.9
  52.1 1.4 %copy-done.9 = bf16[8,1040,128]{2,1,0:T(8,128)(2,1)} copy-done((bf16[8,1040,128]{2,1,0:T(8,128)(2,1)}, bf16[8,1040,128]{2,1,0:T(8,128)(2,1)S(1)}, u32[]{:S(2)}) %copy-start.9) | copy-done | bytes 2129944
  53.5 14.7 %all-to-all-done.2.kv_ref = bf16[8,128,768]{2,1,0:T(8,128)(2,1)} async-done(((bf16[8,128,768]{2,1,0:T(8,128)(2,1)}), bf16[8,128,768]{2,1,0:T(8,128)(2,1)}, u32[]{:S(2)}, u32[]{:S(2)}) %all-to-all-start.2) | async-done | bytes 1572896 | tf_op jit(solution)/shard_map/all_to_all | solution.py:45
  68.2 1.6 %copy-done.10 = bf16[8,1040,128]{2,1,0:T(8,128)(2,1)S(1)} copy-done((bf16[8,1040,128]{2,1,0:T(8,128)(2,1)S(1)}, bf16[8,1040,128]{2,1,0:T(8,128)(2,1)}, u32[]{:S(2)}) %copy-start.10) | copy-done | bytes 2129944
  69.8 17.3 %attention.1 = (bf16[8,512,128]{2,1,0:T(8,128)(2,1)S(1)}, bf16[8,512,128]{2,1,0:T(8,128)(2,1)S(1)}, bf16[8,128,256]{2,1,0:T(8,128)(2,1)S(1)}) custom-call(bf16[8,128,768]{2,1,0:T(8,128)(2,1)} %all-to-all-done.2.kv_ref, bf16[8,1040,128]{2,1,0:T(8,128)(2,1)S(1)} %copy-done.10), custom_call_target="tpu_custom_call" | custom-call | flops 6442450944 | bytes 8388608 | tf_op jit(solution)/shard_map/attention/pallas_call | solution.py:30
  87.1 4.2 %back.1 = bf16[8,288,128]{2,1,0:T(8,128)(2,1)S(1)} custom-call(s32[2]{0:T(128)S(1)} %copy-done.19, s32[1]{0:T(128)} %bitcast.me_ref, bf16[8,384,128]{2,1,0:T(8,128)(2,1)S(1)} %copy-done.1, bf16[8,512,128]{2,1,0:T(8,128)(2,1)S(1)} %get-tuple-element.25.att_ref, bf16[8,512,128]{2,1,0:T(8,128)(2,1)S(1)} %get-tuple-element.26.gq_ref, ...), custom_call_target="tpu_custom_call" | custom-call | flops 503316480 | bytes 8388608 | tf_op jit(solution)/shard_map/back/pallas_call | solution.py:30
  91.4 1.0 copy-done.5
  92.4 0.8 copy-done.8
  93.2 0.8 copy-done.11
  94.0 3.6 %all-to-all-start.3 = ((bf16[8,288,128]{2,1,0:T(8,128)(2,1)}), bf16[8,288,128]{2,1,0:T(8,128)(2,1)S(1)}, u32[]{:S(2)}, u32[]{:S(2)}) async-start(bf16[8,288,128]{2,1,0:T(8,128)(2,1)} %copy-done.8), calls=%async_computation.3 | async-start | bytes 1179648 | tf_op jit(solution)/shard_map/all_to_all | solution.py:45
  97.6 1.4 %copy-done.4 = bf16[512,1536]{1,0:T(8,128)(2,1)S(1)} copy-done((bf16[512,1536]{1,0:T(8,128)(2,1)S(1)}, bf16[512,1536]{1,0:T(8,128)(2,1)}, u32[]{:S(2)}) %copy-start.4) | copy-done | bytes 1572888
  99.0 1.0 copy-done.16
  100.0 1.4 %output.1 = bf16[128,1536]{1,0:T(8,128)(2,1)} custom-call(s32[1]{0:T(128)} %bitcast.me_ref, bf16[128,1536]{1,0:T(8,128)(2,1)S(1)} %copy-done.16, bf16[8,512,128]{2,1,0:T(8,128)(2,1)S(1)} %get-tuple-element.25.att_ref, bf16[512,1536]{1,0:T(8,128)(2,1)S(1)} %copy-done.4), custom_call_target="tpu_custom_call" | custom-call | flops 201326592 | bytes 3145728 | tf_op jit(solution)/shard_map/output/pallas_call | solution.py:30
  101.4 0.1 copy-done.13
  101.5 1.5 %weights.1 = (bf16[192,512]{1,0:T(8,128)(2,1)}, bf16[192,256]{1,0:T(8,128)(2,1)}) custom-call(bf16[8,192,128]{2,1,0:T(8,128)(2,1)S(1)} %copy-done.13, bf16[8,512,128]{2,1,0:T(8,128)(2,1)S(1)} %copy-done.6, bf16[8,128,256]{2,1,0:T(8,128)(2,1)S(1)} %copy-done.12), custom_call_target="tpu_custom_call" | custom-call | flops 301989888 | bytes 4194304 | tf_op jit(solution)/shard_map/weights/pallas_call | solution.py:30
  102.9 4.7 %all-to-all-done.3.x_ref = bf16[8,288,128]{2,1,0:T(8,128)(2,1)S(1)} async-done(((bf16[8,288,128]{2,1,0:T(8,128)(2,1)}), bf16[8,288,128]{2,1,0:T(8,128)(2,1)S(1)}, u32[]{:S(2)}, u32[]{:S(2)}) %all-to-all-start.3) | async-done | bytes 589856 | tf_op jit(solution)/shard_map/all_to_all | solution.py:45
  107.7 1.3 %last.1 = (bf16[128,1536]{1,0:T(8,128)(2,1)}, bf16[64,1536]{1,0:T(8,128)(2,1)}) custom-call(bf16[8,288,128]{2,1,0:T(8,128)(2,1)S(1)} %all-to-all-done.3.x_ref), custom_call_target="tpu_custom_call" | custom-call | bytes 2097152 | tf_op jit(solution)/shard_map/last/pallas_call | solution.py:30
  (28 shorter events, 0.0 us)
Async XLA Ops:
  0.6 8.7 %copy-start.20 = (f32[128,4]{0,1:T(4,128)S(1)}, f32[128,4]{0,1:T(4,128)}, u32[]{:S(2)}) copy-start(f32[128,4]{0,1:T(4,128)} %param.18) | copy-start | bytes 6148
  3.1 6.2 %copy-start.3 = (bf16[512,1536]{1,0:T(8,128)(2,1)S(1)}, bf16[512,1536]{1,0:T(8,128)(2,1)}, u32[]{:S(2)}) copy-start(bf16[512,1536]{1,0:T(8,128)(2,1)} %wout_ref.3) | copy-start | bytes 4718596
  3.2 18.9 %all-to-all-start = ((bf16[8,384,128]{2,1,0:T(8,128)(2,1)}), bf16[8,384,128]{2,1,0:T(8,128)(2,1)S(1)}, u32[]{:S(2)}, u32[]{:S(2)}) async-start(bf16[8,384,128]{2,1,0:T(8,128)(2,1)} %flip.1), calls=%async_computation | async-start | bytes 1572864 | tf_op jit(solution)/shard_map/all_to_all | solution.py:45
  9.4 1.0 copy-start.14
  10.4 0.9 copy-start.18
  12.4 16.1 %collective-permute-start.3 = (bf16[576,128]{1,0:T(8,128)(2,1)S(1)}, bf16[576,128]{1,0:T(8,128)(2,1)}, u32[]{:S(2)}, u32[]{:S(2)}) collective-permute-start(bf16[576,128]{1,0:T(8,128)(2,1)S(1)} %early.1.refs_0_), channel_id=1, source_target_pairs={{0,128},{32,160},{64,192},{96,224},{128,0},{160,32},{192,64},{224,... | collective-permute-start | bytes 442376 | tf_op jit(solution)/shard_map/ppermute | solution.py:429
  14.5 14.0 %collective-permute-start.2 = (bf16[576,128]{1,0:T(8,128)(2,1)S(1)}, bf16[576,128]{1,0:T(8,128)(2,1)}, u32[]{:S(2)}, u32[]{:S(2)}) collective-permute-start(bf16[576,128]{1,0:T(8,128)(2,1)S(1)} %early.1.refs_0_), channel_id=1, source_target_pairs={{0,64},{32,96},{64,0},{96,32},{128,192},{160,224},{192,128},{224,1... | collective-permute-start | bytes 442376 | tf_op jit(solution)/shard_map/ppermute | solution.py:427
  17.5 11.0 %collective-permute-start.1 = (bf16[576,128]{1,0:T(8,128)(2,1)S(1)}, bf16[576,128]{1,0:T(8,128)(2,1)}, u32[]{:S(2)}, u32[]{:S(2)}) collective-permute-start(bf16[576,128]{1,0:T(8,128)(2,1)S(1)} %early.1.refs_0_), channel_id=1, source_target_pairs={{0,96},{32,0},{64,32},{96,64},{128,224},{160,128},{192,160},{224,1... | collective-permute-start | bytes 442376 | tf_op jit(solution)/shard_map/ppermute | solution.py:427
  18.6 9.9 %collective-permute-start = (bf16[576,128]{1,0:T(8,128)(2,1)S(1)}, bf16[576,128]{1,0:T(8,128)(2,1)}, u32[]{:S(2)}, u32[]{:S(2)}) collective-permute-start(bf16[576,128]{1,0:T(8,128)(2,1)S(1)} %early.1.refs_0_), channel_id=1, source_target_pairs={{0,32},{32,64},{64,96},{96,0},{128,160},{160,192},{192,224},{224,1... | collective-permute-start | bytes 442376 | tf_op jit(solution)/shard_map/ppermute | solution.py:427
  22.1 0.9 copy-start
  28.5 13.2 %all-to-all-start.1 = ((bf16[8,192,128]{2,1,0:T(8,128)(2,1)}), bf16[8,192,128]{2,1,0:T(8,128)(2,1)S(1)}, u32[]{:S(2)}, u32[]{:S(2)}) async-start(bf16[8,192,128]{2,1,0:T(8,128)(2,1)} %get-tuple-element.21.x_ref), calls=%async_computation.1 | async-start | bytes 786432 | tf_op jit(solution)/shard_map/all_to_all | solution.py:45
  32.4 13.4 %collective-permute-start.6 = (bf16[576,128]{1,0:T(8,128)(2,1)}, bf16[576,128]{1,0:T(8,128)(2,1)S(1)}, u32[]{:S(2)}, u32[]{:S(2)}) collective-permute-start(bf16[576,128]{1,0:T(8,128)(2,1)} %collective-permute-done.3.refs_4_), channel_id=1, source_target_pairs={{0,64},{32,96},{64,0},{96,32},{128,192},{160,224},{192,128},{224,1... | collective-permute-start | bytes 442376 | tf_op jit(solution)/shard_map/ppermute | solution.py:442
  35.9 9.9 %collective-permute-start.5 = (bf16[576,128]{1,0:T(8,128)(2,1)}, bf16[576,128]{1,0:T(8,128)(2,1)S(1)}, u32[]{:S(2)}, u32[]{:S(2)}) collective-permute-start(bf16[576,128]{1,0:T(8,128)(2,1)} %collective-permute-done.1.refs_2_), channel_id=1, source_target_pairs={{0,128},{32,160},{64,192},{96,224},{128,0},{160,32},{192,64},{224,... | collective-permute-start | bytes 442376 | tf_op jit(solution)/shard_map/ppermute | solution.py:441
  37.4 8.5 %collective-permute-start.4 = (bf16[576,128]{1,0:T(8,128)(2,1)}, bf16[576,128]{1,0:T(8,128)(2,1)S(1)}, u32[]{:S(2)}, u32[]{:S(2)}) collective-permute-start(bf16[576,128]{1,0:T(8,128)(2,1)} %collective-permute-done.refs_1_), channel_id=1, source_target_pairs={{0,128},{32,160},{64,192},{96,224},{128,0},{160,32},{192,64},{224,... | collective-permute-start | bytes 442376 | tf_op jit(solution)/shard_map/ppermute | solution.py:441
  41.7 0.7 copy-start.21
  45.9 22.3 %all-to-all-start.2 = ((bf16[8,128,768]{2,1,0:T(8,128)(2,1)}), bf16[8,128,768]{2,1,0:T(8,128)(2,1)}, u32[]{:S(2)}, u32[]{:S(2)}) async-start(bf16[8,128,768]{2,1,0:T(8,128)(2,1)} %get-tuple-element.24), calls=%async_computation.2 | async-start | bytes 3145728 | tf_op jit(solution)/shard_map/all_to_all | solution.py:45
  52.1 1.4 %copy-start.9 = (bf16[8,1040,128]{2,1,0:T(8,128)(2,1)}, bf16[8,1040,128]{2,1,0:T(8,128)(2,1)S(1)}, u32[]{:S(2)}) copy-start(bf16[8,1040,128]{2,1,0:T(8,128)(2,1)S(1)} %query.1.pack_ref) | copy-start | bytes 6389764
  53.5 33.6 %copy-start.1 = (bf16[8,384,128]{2,1,0:T(8,128)(2,1)S(1)}, bf16[8,384,128]{2,1,0:T(8,128)(2,1)}, u32[]{:S(2)}) copy-start(bf16[8,384,128]{2,1,0:T(8,128)(2,1)} %copy-done) | copy-start | bytes 2359300
  53.5 33.6 %copy-start.2 = (bf16[1536,512]{1,0:T(8,128)(2,1)S(1)}, bf16[1536,512]{1,0:T(8,128)(2,1)}, u32[]{:S(2)}) copy-start(bf16[1536,512]{1,0:T(8,128)(2,1)} %wq_ref.1) | copy-start | bytes 4718596
  68.2 1.6 %copy-start.10 = (bf16[8,1040,128]{2,1,0:T(8,128)(2,1)S(1)}, bf16[8,1040,128]{2,1,0:T(8,128)(2,1)}, u32[]{:S(2)}) copy-start(bf16[8,1040,128]{2,1,0:T(8,128)(2,1)} %copy-done.9) | copy-start | bytes 6389764
  69.8 17.3 %copy-start.7 = (bf16[1536,256]{1,0:T(8,128)(2,1)S(1)}, bf16[1536,256]{1,0:T(8,128)(2,1)}, u32[]{:S(2)}) copy-start(bf16[1536,256]{1,0:T(8,128)(2,1)} %wkv_ref.1) | copy-start | bytes 2359300
  69.8 17.3 %copy-start.15 = (bf16[2,8,192,128]{3,2,1,0:T(8,128)(2,1)S(1)}, bf16[2,8,192,128]{3,2,1,0:T(8,128)(2,1)}, u32[]{:S(2)}) copy-start(bf16[2,8,192,128]{3,2,1,0:T(8,128)(2,1)} %get-tuple-element.28.slope_ref) | copy-start | bytes 2359300
  69.8 17.3 %copy-start.17 = (f32[2,3,1536]{2,0,1:T(2,128)S(1)}, f32[2,3,1536]{2,0,1:T(2,128)}, u32[]{:S(2)}) copy-start(f32[2,3,1536]{2,0,1:T(2,128)} %param.12) | copy-start | bytes 110596
  69.8 17.4 %copy-start.19 = (s32[2]{0:T(128)S(1)}, s32[2]{0:T(128)}, u32[]{:S(2)}) copy-start(s32[2]{0:T(128)} %dil_ref.3) | copy-start | bytes 28
  91.4 1.0 copy-start.5
  92.4 0.8 copy-start.8
  93.2 0.8 copy-start.11
  94.0 13.7 %all-to-all-start.3 = ((bf16[8,288,128]{2,1,0:T(8,128)(2,1)}), bf16[8,288,128]{2,1,0:T(8,128)(2,1)S(1)}, u32[]{:S(2)}, u32[]{:S(2)}) async-start(bf16[8,288,128]{2,1,0:T(8,128)(2,1)} %copy-done.8), calls=%async_computation.3 | async-start | bytes 1179648 | tf_op jit(solution)/shard_map/all_to_all | solution.py:45
  97.6 1.4 %copy-start.4 = (bf16[512,1536]{1,0:T(8,128)(2,1)S(1)}, bf16[512,1536]{1,0:T(8,128)(2,1)}, u32[]{:S(2)}) copy-start(bf16[512,1536]{1,0:T(8,128)(2,1)} %wout_ref.3) | copy-start | bytes 4718596
  99.0 1.0 copy-start.16
  100.0 1.4 %copy-start.6 = (bf16[8,512,128]{2,1,0:T(8,128)(2,1)S(1)}, bf16[8,512,128]{2,1,0:T(8,128)(2,1)}, u32[]{:S(2)}) copy-start(bf16[8,512,128]{2,1,0:T(8,128)(2,1)} %copy-done.5) | copy-start | bytes 3145732
  100.0 1.4 %copy-start.12 = (bf16[8,128,256]{2,1,0:T(8,128)(2,1)S(1)}, bf16[8,128,256]{2,1,0:T(8,128)(2,1)}, u32[]{:S(2)}) copy-start(bf16[8,128,256]{2,1,0:T(8,128)(2,1)} %copy-done.11) | copy-start | bytes 1572868
  100.0 1.5 %copy-start.13 = (bf16[8,192,128]{2,1,0:T(8,128)(2,1)S(1)}, bf16[8,192,128]{2,1,0:T(8,128)(2,1)}, u32[]{:S(2)}) copy-start(bf16[8,192,128]{2,1,0:T(8,128)(2,1)} %get-tuple-element.21.x_ref) | copy-start | bytes 1179652

commit v2 on v1

--- a/solution.py
+++ b/solution.py
@@ -217,23 +217,23 @@
         pick = jnp.where(same_head & (row < 96) & (target == -8 * s), F32(1.0), F32(0.0))
         mirrored += nn(cells_ref[s], pick.astype(BF16))
     lane = lax.broadcasted_iota(jnp.int32, (64, 128), 1)
+    both = []
     for h in range(4):
         one = mirrored[:, 128 * h : 128 * h + 128]
         other = jnp.concatenate([one, one], axis=0).T
         bias = 0.5 * (one + other[:64, :]) * F32(128.0**0.5)
         hi = bias.astype(BF16).astype(F32)
-        both = jnp.where(lane < 64, hi, bias - hi).astype(BF16)
-        for s in range(count):
-            wide = both[8 * s : 8 * s + 8].astype(F32)
-            wide = jnp.broadcast_to(wide[:, None, :], (8, POOL, 128)).reshape(128, 128)
-            pack_ref[s, 512 + 128 * h : 640 + 128 * h, :] = wide.astype(BF16)
+        both.append(jnp.where(lane < 64, hi, bias - hi))
+    for s in range(count):
+        rows = jnp.concatenate([b[8 * s : 8 * s + 8] for b in both], axis=0)
+        pack_ref[s, 512:544, :] = rows.astype(BF16)
     for s in range(count):
         corner = cells_ref[s, 0:1, 127:128].astype(F32)
-        pack_ref[s, 1024:, :] = jnp.broadcast_to(corner, (16, 128)).astype(BF16)
+        pack_ref[s, 544:, :] = jnp.broadcast_to(corner, (16, 128)).astype(BF16)
 
 
 def attention_body(
-    kv_ref, pack_ref, att_ref, gq_ref, out_ref,
+    kv_ref, pack_ref, att_ref, gq_ref,
     sum_ref, kx_ref, v_ref, kt_ref, vt_ref, qx_ref, s_ref, sl_ref, pb_ref, cb_ref,
 ):
     scale = F32(128.0**-0.5)
@@ -241,16 +241,18 @@
     length = count * 128
     for s in range(count):
         rows = slice(128 * s, 128 * s + 128)
-        level = pack_ref[s, 1024:1025, 0:1].astype(F32) * CLIP_LEVEL
+        level = pack_ref[s, 544:560, :][0:1, 0:1].astype(F32) * CLIP_LEVEL
         plain = jnp.clip(kv_ref[s, :, :256].astype(F32), -level, level)
         kx_ref[rows, :128] = plain[:, :128].astype(BF16)
         v_ref[rows, :] = plain[:, 128:].astype(BF16)
         kt_ref[:, rows] = plain[:, :128].T.astype(BF16)
         vt_ref[:, rows] = plain[:, 128:].T.astype(BF16)
+        bias = pack_ref[s, 512:544, :].astype(F32)
         for h in range(4):
             here = slice(128 * h, 128 * h + 128)
             qx_ref[s, here, :128] = kv_ref[s, :, 256 + 128 * h : 384 + 128 * h]
-            qx_ref[s, here, 128:] = pack_ref[s, 512 + 128 * h : 640 + 128 * h, :]
+            wide = jnp.broadcast_to(bias[8 * h : 8 * h + 8][:, None, :], (8, POOL, 128))
+            qx_ref[s, here, 128:] = wide.reshape(128, 128).astype(BF16)
     row = lax.broadcasted_iota(jnp.int32, (length, 128), 0)
     lane = lax.broadcasted_iota(jnp.int32, (length, 128), 1)
     kx_ref[:, 128:] = jnp.where(lane % 64 == row // POOL, F32(1.0), F32(0.0)).astype(BF16)
@@ -312,11 +314,13 @@
     lax.fori_loop(0, count // RUN, step, 0)
     side = lax.broadcasted_iota(jnp.int32, (128, 256), 1)
     for s in range(count):
-        level = pack_ref[s, 1024:1025, 0:1].astype(F32) * CLIP_LEVEL
+        level = pack_ref[s, 544:560, :][0:1, 0:1].astype(F32) * CLIP_LEVEL
         inside = jnp.abs(kv_ref[s, :, :256].astype(F32)) <= level
         part = sum_ref[128 * s : 128 * s + 128, :]
         part = jnp.where(side < 128, part * scale, part)
-        out_ref[s] = jnp.where(inside, part, 0.0).astype(BF16)
+        part = jnp.where(inside, part, 0.0).astype(BF16)
+        gq_ref[s, 512:640, :] = part[:, :128]
+        gq_ref[s, 640:, :] = part[:, 128:]
 
 
 def output_body(me_ref, trunk_ref, att_ref, wout_ref, out_ref):
@@ -329,7 +333,7 @@
 
 
 def back_body(
-    dil_ref, me_ref, x_ref, att_ref, gq_ref, gkv_ref, wq_ref, wkv_ref, taps_ref, slope_ref,
+    dil_ref, me_ref, x_ref, att_ref, gq_ref, wq_ref, wkv_ref, taps_ref, slope_ref,
     out_ref, g_ref, turn_ref,
 ):
     offset = take_taps(me_ref[0], taps_ref, turn_ref)
@@ -339,7 +343,8 @@
     grad_out = jnp.zeros((channels, 512), F32)
     for s in range(count):
         turned = x_ref[s, channels:, :]
-        g_ref[s] = turned.astype(F32) + nn(my_wq, gq_ref[s]) + nt(my_wkv, gkv_ref[s])
+        g_ref[s] = turned.astype(F32) + nn(my_wq, gq_ref[s, :512, :])
+        g_ref[s] += nt(my_wkv[:, :128], gq_ref[s, 512:640, :]) + nt(my_wkv[:, 128:], gq_ref[s, 640:, :])
         grad_out += nt(turned, att_ref[s])
     half = channels // 2
     for s in range(count):
@@ -367,15 +372,17 @@
     lax.fori_loop(0, channels // 16, chunk, 0)
 
 
-def weights_body(x_ref, gq_ref, gkv_ref, gq_out_ref, gkv_out_ref):
+def weights_body(x_ref, gq_ref, gq_out_ref, gkv_out_ref):
     count, channels, _ = x_ref.shape
     first = jnp.zeros(gq_out_ref.shape, F32)
-    second = jnp.zeros(gkv_out_ref.shape, F32)
-    for s in range(count):
-        first += nt(x_ref[s], gq_ref[s])
-        second += nn(x_ref[s], gkv_ref[s])
+    second = [jnp.zeros((channels, 128), F32) for _ in range(2)]
+    for s in range(count):
+        first += nt(x_ref[s], gq_ref[s, :512, :])
+        second[0] += nn(x_ref[s], gq_ref[s, 512:640, :])
+        second[1] += nn(x_ref[s], gq_ref[s, 640:, :])
     gq_out_ref[...] = first.astype(BF16)
-    gkv_out_ref[...] = second.astype(BF16)
+    gkv_out_ref[:, :128] = second[0].astype(BF16)
+    gkv_out_ref[:, 128:] = second[1].astype(BF16)
 
 
 def last_body(x_ref, grad_ref, gout_ref):
@@ -462,7 +469,7 @@
     columns = columns + other
     (pack,) = call(
         query_body,
-        [((count, 1040, 128), BF16)],
+        [((count, 560, 128), BF16)],
         "query",
         2 * rows * width * 512,
         3 * MIB,
@@ -470,9 +477,9 @@
     )(place, *columns)
 
     heads = (count, 512, 128)
-    attended, grad_q, grad_kv = call(
+    attended, grad_q = call(
         attention_body,
-        [(heads, BF16), (heads, BF16), ((count, rows, 256), BF16)],
+        [(heads, BF16), ((count, 768, 128), BF16)],
         "attention",
         12 * length * length * 512,
         8 * MIB,
@@ -498,7 +505,7 @@
         2 * length * ch * 1280,
         8 * MIB,
         scratch=[pltpu.VMEM(blocks, F32), turn],
-    )(dilations, place, turned, attended, grad_q, grad_kv, w_query, w_keyval, my_taps, slopes)
+    )(dilations, place, turned, attended, grad_q, w_query, w_keyval, my_taps, slopes)
     final = exchange(final)
     grad_query, grad_keyval = call(
         weights_body,
@@ -506,7 +513,7 @@
         "weights",
         2 * length * ch * 768,
         4 * MIB,
-    )(trunk_turned, grad_q, grad_kv)
+    )(trunk_turned, grad_q)
     (output,) = call(output_body, [((rows, width), BF16)], "output", 2 * rows * width * 512, 3 * MIB)(
         place, trunk, attended, w_out
     )

time: 110 us -> 110 us (level)
    unnamed x44 -> x46, local copies, waits for them, and re-layouts: 11.6 us -> 12.1 us
where the time goes in v2:
time: 110 us; the launch traced here: 109 us
  Pallas kernels  39.8 us (36%)
  starting transfers between devices  30.3 us (28%)
  waiting for transfers between devices  25.2 us (23%)
  local copies, waits for them, and re-layouts  12.1 us (11%)
  between operations  1.54 us (1%)
    pallas_call x10, Pallas kernels, run(): pl.pallas_call(body, out_shape=[jax.ShapeDtypeStruct(s, d) for s, d in ou...  39.8 us
    all_to_all x4, waiting for transfers between devices, exchange(): return lax.all_to_all(x, 'seq', split_axis=0, concat_axis=0, tiled=True)  25.2 us
    all_to_all x4, starting transfers between devices, exchange(): return lax.all_to_all(x, 'seq', split_axis=0, concat_axis=0, tiled=True)  17.7 us
    unnamed x46, local copies, waits for them, and re-layouts  12.1 us
    ppermute x3, starting transfers between devices, local(): lax.ppermute(grad_attn, 'seq', around[o])  4.99 us
    ppermute x1, starting transfers between devices, local(): other += [lax.ppermute(other[0], 'seq', around[2])]  3.41 us
  transfers between devices with their start and end apart: 11, of which 4 were waited for; matrix products, arithmetic and copies ran while one was open for 0% of the time, Pallas kernels for 13%

profile of v2, /device:TPU:160, one launch (start us, length us, event | category | flops | bytes accessed | tf_op | source)
XLA Modules:
  0.0 108.9 jit_solution(18155752394984881867)
XLA Ops:
  0.6 2.5 %flip.1 = bf16[8,384,128]{2,1,0:T(8,128)(2,1)} custom-call(bf16[128,1536]{1,0:T(8,128)(2,1)} %tok_hbm.1, bf16[128,1536]{1,0:T(8,128)(2,1)} %cot_ref.1), custom_call_target="tpu_custom_call" | custom-call | bytes 786432 | tf_op jit(solution)/shard_map/flip/pallas_call | solution.py:30
  3.2 0.0 copy-start.3
  3.2 5.5 %all-to-all-start = ((bf16[8,384,128]{2,1,0:T(8,128)(2,1)}), bf16[8,384,128]{2,1,0:T(8,128)(2,1)S(1)}, u32[]{:S(2)}, u32[]{:S(2)}) async-start(bf16[8,384,128]{2,1,0:T(8,128)(2,1)} %flip.1), calls=%async_computation | async-start | bytes 1572864 | tf_op jit(solution)/shard_map/all_to_all | solution.py:45
  9.4 0.0 copy-start.10
  9.4 1.0 copy-done.10
  10.4 0.9 copy-done.20
  11.3 1.1 early.1.refs_0_
  12.4 2.1 %collective-permute-start.3 = (bf16[576,128]{1,0:T(8,128)(2,1)S(1)}, bf16[576,128]{1,0:T(8,128)(2,1)}, u32[]{:S(2)}, u32[]{:S(2)}) collective-permute-start(bf16[576,128]{1,0:T(8,128)(2,1)S(1)} %early.1.refs_0_), channel_id=1, source_target_pairs={{0,128},{32,160},{64,192},{96,224},{128,0},{160,32},{192,64},{224,... | collective-permute-start | bytes 442376 | tf_op jit(solution)/shard_map/ppermute | solution.py:436
  14.5 3.0 %collective-permute-start.2 = (bf16[576,128]{1,0:T(8,128)(2,1)S(1)}, bf16[576,128]{1,0:T(8,128)(2,1)}, u32[]{:S(2)}, u32[]{:S(2)}) collective-permute-start(bf16[576,128]{1,0:T(8,128)(2,1)S(1)} %early.1.refs_0_), channel_id=1, source_target_pairs={{0,64},{32,96},{64,0},{96,32},{128,192},{160,224},{192,128},{224,1... | collective-permute-start | bytes 442376 | tf_op jit(solution)/shard_map/ppermute | solution.py:434
  17.5 1.2 %collective-permute-start.1 = (bf16[576,128]{1,0:T(8,128)(2,1)S(1)}, bf16[576,128]{1,0:T(8,128)(2,1)}, u32[]{:S(2)}, u32[]{:S(2)}) collective-permute-start(bf16[576,128]{1,0:T(8,128)(2,1)S(1)} %early.1.refs_0_), channel_id=1, source_target_pairs={{0,96},{32,0},{64,32},{96,64},{128,224},{160,128},{192,160},{224,1... | collective-permute-start | bytes 442376 | tf_op jit(solution)/shard_map/ppermute | solution.py:434
  18.6 0.9 collective-permute-start
  19.5 2.6 %all-to-all-done.x_ref = bf16[8,384,128]{2,1,0:T(8,128)(2,1)S(1)} async-done(((bf16[8,384,128]{2,1,0:T(8,128)(2,1)}), bf16[8,384,128]{2,1,0:T(8,128)(2,1)S(1)}, u32[]{:S(2)}, u32[]{:S(2)}) %all-to-all-start) | async-done | bytes 786464 | tf_op jit(solution)/shard_map/all_to_all | solution.py:45
  22.1 0.9 copy-done
  23.0 5.5 %conv.1 = (bf16[8,192,128]{2,1,0:T(8,128)(2,1)}, bf16[2,8,192,128]{3,2,1,0:T(8,128)(2,1)}) custom-call(s32[2]{0:T(128)} %dil_ref.3, s32[1]{0:T(128)} %bitcast.me_ref, bf16[8,384,128]{2,1,0:T(8,128)(2,1)} %copy-done, f32[3,2,1536]{2,1,0:T(2,128)} %bitcast.3), custom_call_target="tpu_custom_call" | custom-call | flops 19660800 | bytes 4194304 | tf_op jit(solution)/shard_map/conv/pallas_call | solution.py:30
  28.5 0.0 collective-permute-done.3.refs_4_
  28.5 0.0 collective-permute-done.2.refs_3_
  28.5 4.1 %all-to-all-start.1 = ((bf16[8,192,128]{2,1,0:T(8,128)(2,1)}), bf16[8,192,128]{2,1,0:T(8,128)(2,1)}, u32[]{:S(2)}, u32[]{:S(2)}) async-start(bf16[8,192,128]{2,1,0:T(8,128)(2,1)} %get-tuple-element.20.x_ref), calls=%async_computation.1 | async-start | bytes 786432 | tf_op jit(solution)/shard_map/all_to_all | solution.py:45
  32.7 3.4 %collective-permute-start.6 = (bf16[576,128]{1,0:T(8,128)(2,1)}, bf16[576,128]{1,0:T(8,128)(2,1)S(1)}, u32[]{:S(2)}, u32[]{:S(2)}) collective-permute-start(bf16[576,128]{1,0:T(8,128)(2,1)} %collective-permute-done.3.refs_4_), channel_id=1, source_target_pairs={{0,64},{32,96},{64,0},{96,32},{128,192},{160,224},{192,128},{224,1... | collective-permute-start | bytes 442376 | tf_op jit(solution)/shard_map/ppermute | solution.py:449
  36.1 1.5 %collective-permute-start.5 = (bf16[576,128]{1,0:T(8,128)(2,1)}, bf16[576,128]{1,0:T(8,128)(2,1)S(1)}, u32[]{:S(2)}, u32[]{:S(2)}) collective-permute-start(bf16[576,128]{1,0:T(8,128)(2,1)} %collective-permute-done.1.refs_2_), channel_id=1, source_target_pairs={{0,128},{32,160},{64,192},{96,224},{128,0},{160,32},{192,64},{224,... | collective-permute-start | bytes 442376 | tf_op jit(solution)/shard_map/ppermute | solution.py:448
  37.5 0.5 collective-permute-start.4
  38.1 3.8 %all-to-all-done.1.x_hbm = bf16[8,192,128]{2,1,0:T(8,128)(2,1)} async-done(((bf16[8,192,128]{2,1,0:T(8,128)(2,1)}), bf16[8,192,128]{2,1,0:T(8,128)(2,1)}, u32[]{:S(2)}, u32[]{:S(2)}) %all-to-all-start.1) | async-done | bytes 393248 | tf_op jit(solution)/shard_map/all_to_all | solution.py:45
  41.9 3.4 %keyval.1 = (bf16[8,128,768]{2,1,0:T(8,128)(2,1)}, bf16[128,1536]{1,0:T(8,128)(2,1)}) custom-call(s32[1]{0:T(128)S(6)} %copy.15.exp_ref, bf16[8,192,128]{2,1,0:T(8,128)(2,1)} %all-to-all-done.1.x_hbm, bf16[1536,256]{1,0:T(8,128)(2,1)} %wkv_ref.1, bf16[1536,512]{1,0:T(8,128)(2,1)} %wq_ref.1), custom_call_target="tpu_custom_call" | custom-call | flops 301989888 | bytes 2097152 | tf_op jit(solution)/shard_map/keyval/pallas_call | solution.py:30
  45.4 0.0 collective-permute-done.6.refs_7_
  45.4 0.0 copy-start.16
  45.4 0.0 copy-start.18
  45.4 0.6 copy-done.16
  46.0 0.0 copy-done.18
  46.1 4.5 %all-to-all-start.2 = ((bf16[8,128,768]{2,1,0:T(8,128)(2,1)}), bf16[8,128,768]{2,1,0:T(8,128)(2,1)}, u32[]{:S(2)}, u32[]{:S(2)}) async-start(bf16[8,128,768]{2,1,0:T(8,128)(2,1)} %get-tuple-element.23), calls=%async_computation.2 | async-start | bytes 3145728 | tf_op jit(solution)/shard_map/all_to_all | solution.py:45
  50.6 0.0 copy-start.17
  50.6 0.9 copy-done.17
  51.5 0.9 copy-done.19
  52.4 1.6 %query.1.pack_ref = bf16[8,560,128]{2,1,0:T(8,128)(2,1)S(1)} custom-call(s32[1]{0:T(128)} %bitcast.me_ref, bf16[576,128]{1,0:T(8,128)(2,1)S(1)} %early.1.refs_0_, bf16[576,128]{1,0:T(8,128)(2,1)} %collective-permute-done.refs_1_, bf16[576,128]{1,0:T(8,128)(2,1)} %collective-permute-done.1.refs_2_, bf16[576,128]{1,0:T(8,128)(2,1)} %collective-permute-done.2.refs_3_, ...), custom_call_target="tpu_custom_call" | custom-call | flops 201326592 | bytes 3145728 | tf_op jit(solution)/shard_map/query/pallas_call | solution.py:30
  54.1 1.0 copy-done.11
  55.1 14.0 %all-to-all-done.2.kv_ref = bf16[8,128,768]{2,1,0:T(8,128)(2,1)} async-done(((bf16[8,128,768]{2,1,0:T(8,128)(2,1)}), bf16[8,128,768]{2,1,0:T(8,128)(2,1)}, u32[]{:S(2)}, u32[]{:S(2)}) %all-to-all-start.2) | async-done | bytes 1572896 | tf_op jit(solution)/shard_map/all_to_all | solution.py:45
  69.0 1.3 %copy-done.12 = bf16[8,560,128]{2,1,0:T(8,128)(2,1)S(1)} copy-done((bf16[8,560,128]{2,1,0:T(8,128)(2,1)S(1)}, bf16[8,560,128]{2,1,0:T(8,128)(2,1)}, u32[]{:S(2)}) %copy-start.12) | copy-done | bytes 1146904
  70.3 17.1 %attention.1 = (bf16[8,512,128]{2,1,0:T(8,128)(2,1)S(1)}, bf16[8,768,128]{2,1,0:T(8,128)(2,1)S(1)}) custom-call(bf16[8,128,768]{2,1,0:T(8,128)(2,1)} %all-to-all-done.2.kv_ref, bf16[8,560,128]{2,1,0:T(8,128)(2,1)S(1)} %copy-done.12), custom_call_target="tpu_custom_call" | custom-call | flops 6442450944 | bytes 8388608 | tf_op jit(solution)/shard_map/attention/pallas_call | solution.py:30
  87.5 4.3 %back.1 = bf16[8,288,128]{2,1,0:T(8,128)(2,1)S(1)} custom-call(s32[2]{0:T(128)S(1)} %copy-done.21, s32[1]{0:T(128)} %bitcast.me_ref, bf16[8,384,128]{2,1,0:T(8,128)(2,1)S(1)} %copy-done.1, bf16[8,512,128]{2,1,0:T(8,128)(2,1)S(1)} %get-tuple-element.24.att_ref, bf16[8,768,128]{2,1,0:T(8,128)(2,1)S(1)} %get-tuple-element.25.gq_ref, ...), custom_call_target="tpu_custom_call" | custom-call | flops 503316480 | bytes 8388608 | tf_op jit(solution)/shard_map/back/pallas_call | solution.py:30
  91.8 1.2 %copy-done.5 = bf16[8,768,128]{2,1,0:T(8,128)(2,1)} copy-done((bf16[8,768,128]{2,1,0:T(8,128)(2,1)}, bf16[8,768,128]{2,1,0:T(8,128)(2,1)S(1)}, u32[]{:S(2)}) %copy-start.5) | copy-done | bytes 1572888
  93.0 0.8 copy-done.8
  93.8 3.6 %all-to-all-start.3 = ((bf16[8,288,128]{2,1,0:T(8,128)(2,1)}), bf16[8,288,128]{2,1,0:T(8,128)(2,1)S(1)}, u32[]{:S(2)}, u32[]{:S(2)}) async-start(bf16[8,288,128]{2,1,0:T(8,128)(2,1)} %copy-done.8), calls=%async_computation.3 | async-start | bytes 1179648 | tf_op jit(solution)/shard_map/all_to_all | solution.py:45
  97.4 1.4 %copy-done.4 = bf16[512,1536]{1,0:T(8,128)(2,1)S(1)} copy-done((bf16[512,1536]{1,0:T(8,128)(2,1)S(1)}, bf16[512,1536]{1,0:T(8,128)(2,1)}, u32[]{:S(2)}) %copy-start.4) | copy-done | bytes 1572888
  98.8 1.0 copy-done.14
  99.8 1.4 %output.1 = bf16[128,1536]{1,0:T(8,128)(2,1)} custom-call(s32[1]{0:T(128)} %bitcast.me_ref, bf16[128,1536]{1,0:T(8,128)(2,1)S(1)} %copy-done.14, bf16[8,512,128]{2,1,0:T(8,128)(2,1)S(1)} %get-tuple-element.24.att_ref, bf16[512,1536]{1,0:T(8,128)(2,1)S(1)} %copy-done.4), custom_call_target="tpu_custom_call" | custom-call | flops 201326592 | bytes 3145728 | tf_op jit(solution)/shard_map/output/pallas_call | solution.py:30
  101.2 0.0 copy-done.6
  101.2 0.1 copy-done.9
  101.3 1.5 %weights.1 = (bf16[192,512]{1,0:T(8,128)(2,1)}, bf16[192,256]{1,0:T(8,128)(2,1)}) custom-call(bf16[8,192,128]{2,1,0:T(8,128)(2,1)S(1)} %copy-done.9, bf16[8,768,128]{2,1,0:T(8,128)(2,1)S(1)} %copy-done.6), custom_call_target="tpu_custom_call" | custom-call | flops 301989888 | bytes 4194304 | tf_op jit(solution)/shard_map/weights/pallas_call | solution.py:30
  102.9 4.8 %all-to-all-done.3.x_ref = bf16[8,288,128]{2,1,0:T(8,128)(2,1)S(1)} async-done(((bf16[8,288,128]{2,1,0:T(8,128)(2,1)}), bf16[8,288,128]{2,1,0:T(8,128)(2,1)S(1)}, u32[]{:S(2)}, u32[]{:S(2)}) %all-to-all-start.3) | async-done | bytes 589856 | tf_op jit(solution)/shard_map/all_to_all | solution.py:45
  107.7 1.3 %last.1 = (bf16[128,1536]{1,0:T(8,128)(2,1)}, bf16[64,1536]{1,0:T(8,128)(2,1)}) custom-call(bf16[8,288,128]{2,1,0:T(8,128)(2,1)S(1)} %all-to-all-done.3.x_ref), custom_call_target="tpu_custom_call" | custom-call | bytes 2097152 | tf_op jit(solution)/shard_map/last/pallas_call | solution.py:30
  (30 shorter events, 0.1 us)
Async XLA Ops:
  0.6 8.7 %copy-start.22 = (f32[128,4]{0,1:T(4,128)S(1)}, f32[128,4]{0,1:T(4,128)}, u32[]{:S(2)}) copy-start(f32[128,4]{0,1:T(4,128)} %param.18) | copy-start | bytes 6148
  3.2 6.2 %copy-start.3 = (bf16[512,1536]{1,0:T(8,128)(2,1)S(1)}, bf16[512,1536]{1,0:T(8,128)(2,1)}, u32[]{:S(2)}) copy-start(bf16[512,1536]{1,0:T(8,128)(2,1)} %wout_ref.3) | copy-start | bytes 4718596
  3.2 18.9 %all-to-all-start = ((bf16[8,384,128]{2,1,0:T(8,128)(2,1)}), bf16[8,384,128]{2,1,0:T(8,128)(2,1)S(1)}, u32[]{:S(2)}, u32[]{:S(2)}) async-start(bf16[8,384,128]{2,1,0:T(8,128)(2,1)} %flip.1), calls=%async_computation | async-start | bytes 1572864 | tf_op jit(solution)/shard_map/all_to_all | solution.py:45
  9.4 1.0 copy-start.10
  10.4 0.9 copy-start.20
  12.4 16.1 %collective-permute-start.3 = (bf16[576,128]{1,0:T(8,128)(2,1)S(1)}, bf16[576,128]{1,0:T(8,128)(2,1)}, u32[]{:S(2)}, u32[]{:S(2)}) collective-permute-start(bf16[576,128]{1,0:T(8,128)(2,1)S(1)} %early.1.refs_0_), channel_id=1, source_target_pairs={{0,128},{32,160},{64,192},{96,224},{128,0},{160,32},{192,64},{224,... | collective-permute-start | bytes 442376 | tf_op jit(solution)/shard_map/ppermute | solution.py:436
  14.5 14.0 %collective-permute-start.2 = (bf16[576,128]{1,0:T(8,128)(2,1)S(1)}, bf16[576,128]{1,0:T(8,128)(2,1)}, u32[]{:S(2)}, u32[]{:S(2)}) collective-permute-start(bf16[576,128]{1,0:T(8,128)(2,1)S(1)} %early.1.refs_0_), channel_id=1, source_target_pairs={{0,64},{32,96},{64,0},{96,32},{128,192},{160,224},{192,128},{224,1... | collective-permute-start | bytes 442376 | tf_op jit(solution)/shard_map/ppermute | solution.py:434
  17.5 11.1 %collective-permute-start.1 = (bf16[576,128]{1,0:T(8,128)(2,1)S(1)}, bf16[576,128]{1,0:T(8,128)(2,1)}, u32[]{:S(2)}, u32[]{:S(2)}) collective-permute-start(bf16[576,128]{1,0:T(8,128)(2,1)S(1)} %early.1.refs_0_), channel_id=1, source_target_pairs={{0,96},{32,0},{64,32},{96,64},{128,224},{160,128},{192,160},{224,1... | collective-permute-start | bytes 442376 | tf_op jit(solution)/shard_map/ppermute | solution.py:434
  18.6 9.9 %collective-permute-start = (bf16[576,128]{1,0:T(8,128)(2,1)S(1)}, bf16[576,128]{1,0:T(8,128)(2,1)}, u32[]{:S(2)}, u32[]{:S(2)}) collective-permute-start(bf16[576,128]{1,0:T(8,128)(2,1)S(1)} %early.1.refs_0_), channel_id=1, source_target_pairs={{0,32},{32,64},{64,96},{96,0},{128,160},{160,192},{192,224},{224,1... | collective-permute-start | bytes 442376 | tf_op jit(solution)/shard_map/ppermute | solution.py:434
  22.1 0.9 copy-start
  28.5 13.4 %all-to-all-start.1 = ((bf16[8,192,128]{2,1,0:T(8,128)(2,1)}), bf16[8,192,128]{2,1,0:T(8,128)(2,1)}, u32[]{:S(2)}, u32[]{:S(2)}) async-start(bf16[8,192,128]{2,1,0:T(8,128)(2,1)} %get-tuple-element.20.x_ref), calls=%async_computation.1 | async-start | bytes 786432 | tf_op jit(solution)/shard_map/all_to_all | solution.py:45
  32.7 12.7 %collective-permute-start.6 = (bf16[576,128]{1,0:T(8,128)(2,1)}, bf16[576,128]{1,0:T(8,128)(2,1)S(1)}, u32[]{:S(2)}, u32[]{:S(2)}) collective-permute-start(bf16[576,128]{1,0:T(8,128)(2,1)} %collective-permute-done.3.refs_4_), channel_id=1, source_target_pairs={{0,64},{32,96},{64,0},{96,32},{128,192},{160,224},{192,128},{224,1... | collective-permute-start | bytes 442376 | tf_op jit(solution)/shard_map/ppermute | solution.py:449
  36.1 9.3 %collective-permute-start.5 = (bf16[576,128]{1,0:T(8,128)(2,1)}, bf16[576,128]{1,0:T(8,128)(2,1)S(1)}, u32[]{:S(2)}, u32[]{:S(2)}) collective-permute-start(bf16[576,128]{1,0:T(8,128)(2,1)} %collective-permute-done.1.refs_2_), channel_id=1, source_target_pairs={{0,128},{32,160},{64,192},{96,224},{128,0},{160,32},{192,64},{224,... | collective-permute-start | bytes 442376 | tf_op jit(solution)/shard_map/ppermute | solution.py:448
  37.5 7.8 %collective-permute-start.4 = (bf16[576,128]{1,0:T(8,128)(2,1)}, bf16[576,128]{1,0:T(8,128)(2,1)S(1)}, u32[]{:S(2)}, u32[]{:S(2)}) collective-permute-start(bf16[576,128]{1,0:T(8,128)(2,1)} %collective-permute-done.refs_1_), channel_id=1, source_target_pairs={{0,128},{32,160},{64,192},{96,224},{128,0},{160,32},{192,64},{224,... | collective-permute-start | bytes 442376 | tf_op jit(solution)/shard_map/ppermute | solution.py:448
  45.4 0.7 copy-start.16
  45.4 0.7 copy-start.18
  46.1 23.0 %all-to-all-start.2 = ((bf16[8,128,768]{2,1,0:T(8,128)(2,1)}), bf16[8,128,768]{2,1,0:T(8,128)(2,1)}, u32[]{:S(2)}, u32[]{:S(2)}) async-start(bf16[8,128,768]{2,1,0:T(8,128)(2,1)} %get-tuple-element.23), calls=%async_computation.2 | async-start | bytes 3145728 | tf_op jit(solution)/shard_map/all_to_all | solution.py:45
  50.6 0.9 copy-start.17
  51.5 0.9 copy-start.19
  54.0 1.0 copy-start.11
  55.1 32.4 %copy-start.1 = (bf16[8,384,128]{2,1,0:T(8,128)(2,1)S(1)}, bf16[8,384,128]{2,1,0:T(8,128)(2,1)}, u32[]{:S(2)}) copy-start(bf16[8,384,128]{2,1,0:T(8,128)(2,1)} %copy-done) | copy-start | bytes 2359300
  55.1 32.4 %copy-start.2 = (bf16[1536,512]{1,0:T(8,128)(2,1)S(1)}, bf16[1536,512]{1,0:T(8,128)(2,1)}, u32[]{:S(2)}) copy-start(bf16[1536,512]{1,0:T(8,128)(2,1)} %wq_ref.1) | copy-start | bytes 4718596
  69.0 1.3 %copy-start.12 = (bf16[8,560,128]{2,1,0:T(8,128)(2,1)S(1)}, bf16[8,560,128]{2,1,0:T(8,128)(2,1)}, u32[]{:S(2)}) copy-start(bf16[8,560,128]{2,1,0:T(8,128)(2,1)} %copy-done.11) | copy-start | bytes 3440644
  70.3 17.2 %copy-start.7 = (bf16[1536,256]{1,0:T(8,128)(2,1)S(1)}, bf16[1536,256]{1,0:T(8,128)(2,1)}, u32[]{:S(2)}) copy-start(bf16[1536,256]{1,0:T(8,128)(2,1)} %wkv_ref.1) | copy-start | bytes 2359300
  70.3 17.2 %copy-start.13 = (bf16[2,8,192,128]{3,2,1,0:T(8,128)(2,1)S(1)}, bf16[2,8,192,128]{3,2,1,0:T(8,128)(2,1)}, u32[]{:S(2)}) copy-start(bf16[2,8,192,128]{3,2,1,0:T(8,128)(2,1)} %get-tuple-element.26.slope_ref) | copy-start | bytes 2359300
  70.3 17.2 %copy-start.15 = (f32[2,3,1536]{2,0,1:T(2,128)S(1)}, f32[2,3,1536]{2,0,1:T(2,128)}, u32[]{:S(2)}) copy-start(f32[2,3,1536]{2,0,1:T(2,128)} %param.12) | copy-start | bytes 110596
  70.3 17.2 %copy-start.21 = (s32[2]{0:T(128)S(1)}, s32[2]{0:T(128)}, u32[]{:S(2)}) copy-start(s32[2]{0:T(128)} %dil_ref.3) | copy-start | bytes 28
  91.8 1.2 %copy-start.5 = (bf16[8,768,128]{2,1,0:T(8,128)(2,1)}, bf16[8,768,128]{2,1,0:T(8,128)(2,1)S(1)}, u32[]{:S(2)}) copy-start(bf16[8,768,128]{2,1,0:T(8,128)(2,1)S(1)} %get-tuple-element.25.gq_ref) | copy-start | bytes 4718596
  93.0 0.8 copy-start.8
  93.8 13.8 %all-to-all-start.3 = ((bf16[8,288,128]{2,1,0:T(8,128)(2,1)}), bf16[8,288,128]{2,1,0:T(8,128)(2,1)S(1)}, u32[]{:S(2)}, u32[]{:S(2)}) async-start(bf16[8,288,128]{2,1,0:T(8,128)(2,1)} %copy-done.8), calls=%async_computation.3 | async-start | bytes 1179648 | tf_op jit(solution)/shard_map/all_to_all | solution.py:45
  97.4 1.4 %copy-start.4 = (bf16[512,1536]{1,0:T(8,128)(2,1)S(1)}, bf16[512,1536]{1,0:T(8,128)(2,1)}, u32[]{:S(2)}) copy-start(bf16[512,1536]{1,0:T(8,128)(2,1)} %wout_ref.3) | copy-start | bytes 4718596
  98.8 1.0 copy-start.14
  99.8 1.4 %copy-start.6 = (bf16[8,768,128]{2,1,0:T(8,128)(2,1)S(1)}, bf16[8,768,128]{2,1,0:T(8,128)(2,1)}, u32[]{:S(2)}) copy-start(bf16[8,768,128]{2,1,0:T(8,128)(2,1)} %copy-done.5) | copy-start | bytes 4718596
  99.8 1.5 %copy-start.9 = (bf16[8,192,128]{2,1,0:T(8,128)(2,1)S(1)}, bf16[8,192,128]{2,1,0:T(8,128)(2,1)}, u32[]{:S(2)}) copy-start(bf16[8,192,128]{2,1,0:T(8,128)(2,1)} %get-tuple-element.20.x_ref) | copy-start | bytes 1179652
